TPU v7x, 32 devices: a whole 2x2x4 slice. The times are simulated.
32 devices in a mesh: dp: 4 (over x, core), fsdp: 8 (over z, y).
Axes of the slice: x: 2, y: 2, z: 4, core: 2. Of those that a mesh axis runs over, the one named last changes fastest.
Arguments:
- tokens: bfloat16 [30720, 512], P(('dp', 'fsdp')), may hold values from -6 to 6
- frames: int32 [6144], P(('dp', 'fsdp')), may hold values from 2 to 5, as said below
- norm1_gain: float32 [512], P(('dp', 'fsdp')), may hold values from 0.1 to 1.9
- norm1_bias: float32 [512], P(('dp', 'fsdp')), may hold values from -1.75 to 1.75
- qkv_weight: float32 [786432], P(('dp', 'fsdp')), may hold values from -0.25 to 0.25
- qv_bias: float32 [1024], P(('dp', 'fsdp')), may hold values from -1.75 to 1.75
- out_weight: float32 [262144], P(('dp', 'fsdp')), may hold values from -0.375 to 0.375
- out_bias: float32 [512], P(('dp', 'fsdp')), may hold values from -1.75 to 1.75
- norm2_gain: float32 [512], P(('dp', 'fsdp')), may hold values from 0.1 to 1.9
- norm2_bias: float32 [512], P(('dp', 'fsdp')), may hold values from -1.75 to 1.75
- up_weight: float32 [1048576], P(('dp', 'fsdp')), may hold values from -0.25 to 0.25
- up_bias: float32 [2048], P(('dp', 'fsdp')), may hold values from -1.75 to 1.75
- down_weight: float32 [1048576], P(('dp', 'fsdp')), may hold values from -0.125 to 0.125
- down_bias: float32 [512], P(('dp', 'fsdp')), may hold values from -1.75 to 1.75
- cotangent: bfloat16 [30720, 512], P(('dp', 'fsdp')), may hold values from -6 to 6
Outputs:
- mixed: bfloat16 [30720, 512], P(('dp', 'fsdp'))
- tokens_grad: bfloat16 [30720, 512], P(('dp', 'fsdp'))
- grad_norm1_gain: float32 [512], P(('dp', 'fsdp'))
- grad_norm1_bias: float32 [512], P(('dp', 'fsdp'))
- grad_qkv_weight: float32 [786432], P(('dp', 'fsdp'))
- grad_qv_bias: float32 [1024], P(('dp', 'fsdp'))
- grad_out_weight: float32 [262144], P(('dp', 'fsdp'))
- grad_out_bias: float32 [512], P(('dp', 'fsdp'))
- grad_norm2_gain: float32 [512], P(('dp', 'fsdp'))
- grad_norm2_bias: float32 [512], P(('dp', 'fsdp'))
- grad_up_weight: float32 [1048576], P(('dp', 'fsdp'))
- grad_up_bias: float32 [2048], P(('dp', 'fsdp'))
- grad_down_weight: float32 [1048576], P(('dp', 'fsdp'))
- grad_down_bias: float32 [512], P(('dp', 'fsdp'))
Inputs may be any that keep to these rules, and one draw needn't show every extreme that they name: Each sequence has 2, 3 or 5 valid frames; both ends occur.
All inputs are finite; a program needn't handle non-finite values.
Results may differ from a plain program's by a relative error of at most 0.011.
Values may be sent and summed in bfloat16 or wider, within the bound.
A program may use at most 128 MiB of HBM per device.

v0:
```python
import math

import jax
import jax.numpy as jnp
from jax import lax
from jax.sharding import PartitionSpec as P

D = 512
HEADS = 8
HEAD_DIM = 64
FF = 2048
FRAMES = 5


EPSILON = 1e-05
PRECISE = lax.Precision.HIGHEST


def normalize(values, gain, shift):
    centered = values - jnp.mean(values, axis=-1, keepdims=True)
    variance = jnp.mean(centered * centered, axis=-1, keepdims=True)
    return centered * lax.rsqrt(variance + EPSILON) * gain + shift


def attend(queries, keys_in, values_in, frames):
    span = queries.shape[1]
    scale = 1.0 / math.sqrt(queries.shape[3])
    scores = jnp.einsum("sthe,suhe->shtu", queries, keys_in, precision=PRECISE) * scale
    slots = jnp.arange(span, dtype=jnp.int32)
    causal = slots[None, :] <= slots[:, None]
    living = slots[None, :] < frames[:, None]
    allowed = causal[None, None, :, :] & living[:, None, None, :]
    scores = jnp.where(allowed, scores, -1e30)
    highest = jnp.max(scores, axis=-1, keepdims=True)
    weights = jnp.exp(scores - highest)
    weights = weights / jnp.sum(weights, axis=-1, keepdims=True)
    return jnp.einsum("shtu,suhe->sthe", weights, values_in, precision=PRECISE)


def product(left, right):
    return jnp.dot(left, right, preferred_element_type=jnp.float32)


def product_back(left, right):
    return lax.dot_general(
        left, right, (((1,), (1,)), ((), ())), preferred_element_type=jnp.float32
    )


def product_rows(left, right):
    return lax.dot_general(
        left, right, (((0,), (0,)), ((), ())), preferred_element_type=jnp.float32
    )


def attention_pieces(gathered):
    return (
        gathered[0].astype(jnp.float32),
        gathered[1].astype(jnp.float32),
        gathered[2].reshape(D, 3 * D),
        gathered[3].astype(jnp.float32),
        gathered[4].reshape(D, D),
        gathered[5].astype(jnp.float32),
    )


def feed_pieces(gathered):
    return (
        gathered[0].astype(jnp.float32),
        gathered[1].astype(jnp.float32),
        gathered[2].reshape(D, FF),
        gathered[3].astype(jnp.float32),
        gathered[4].reshape(FF, D),
        gathered[5].astype(jnp.float32),
    )


def local(
    tokens,
    frames,
    norm1_gain,
    norm1_bias,
    qkv_weight,
    qv_bias,
    out_weight,
    out_bias,
    norm2_gain,
    norm2_bias,
    up_weight,
    up_bias,
    down_weight,
    down_bias,
    cotangent,
):
    attn_low = tuple(
        (
            piece.astype(jnp.bfloat16)
            for piece in (norm1_gain, norm1_bias, qkv_weight, qv_bias, out_weight, out_bias)
        )
    )
    feed_low = tuple(
        (
            piece.astype(jnp.bfloat16)
            for piece in (norm2_gain, norm2_bias, up_weight, up_bias, down_weight, down_bias)
        )
    )
    count = tokens.shape[0]
    seqs_here = count // FRAMES
    states = tokens.astype(jnp.float32)
    attn_whole = (
        lax.all_gather(attn_low[0], ("dp", "fsdp"), axis=0, tiled=True),
        lax.all_gather(attn_low[1], ("dp", "fsdp"), axis=0, tiled=True),
        lax.all_gather(attn_low[2], ("dp", "fsdp"), axis=0, tiled=True),
        lax.all_gather(attn_low[3], ("dp", "fsdp"), axis=0, tiled=True),
        lax.all_gather(attn_low[4], ("dp", "fsdp"), axis=0, tiled=True),
        lax.all_gather(attn_low[5], ("dp", "fsdp"), axis=0, tiled=True),
    )
    gain_one, shift_one, qkv_matrix, pair_bias, proj_matrix, proj_shift = attention_pieces(
        attn_whole
    )
    first = normalize(states, gain_one, shift_one).astype(jnp.bfloat16)
    bias_full = jnp.concatenate([pair_bias[:D], jnp.zeros((D,), jnp.float32), pair_bias[D:]])
    packed = (product(first, qkv_matrix) + bias_full).astype(jnp.bfloat16)
    split_view = packed.reshape(seqs_here, FRAMES, 3, HEADS, HEAD_DIM).astype(jnp.float32)
    queries = split_view[:, :, 0]
    keys_in = split_view[:, :, 1]
    values_in = split_view[:, :, 2]
    context = attend(queries, keys_in, values_in, frames).reshape(count, D).astype(jnp.bfloat16)
    middle = states + product(context, proj_matrix) + proj_shift
    feed_whole = (
        lax.all_gather(feed_low[0], ("dp", "fsdp"), axis=0, tiled=True),
        lax.all_gather(feed_low[1], ("dp", "fsdp"), axis=0, tiled=True),
        lax.all_gather(feed_low[2], ("dp", "fsdp"), axis=0, tiled=True),
        lax.all_gather(feed_low[3], ("dp", "fsdp"), axis=0, tiled=True),
        lax.all_gather(feed_low[4], ("dp", "fsdp"), axis=0, tiled=True),
        lax.all_gather(feed_low[5], ("dp", "fsdp"), axis=0, tiled=True),
    )
    gain_two, shift_two, up_matrix, up_shift, down_matrix, down_shift = feed_pieces(feed_whole)
    second = normalize(middle, gain_two, shift_two).astype(jnp.bfloat16)
    lifted = product(second, up_matrix) + up_shift
    activated = jax.nn.gelu(lifted).astype(jnp.bfloat16)
    mixed = (middle + product(activated, down_matrix) + down_shift).astype(jnp.bfloat16)
    feed_again = (
        lax.all_gather(feed_low[0], ("dp", "fsdp"), axis=0, tiled=True),
        lax.all_gather(feed_low[1], ("dp", "fsdp"), axis=0, tiled=True),
        lax.all_gather(feed_low[2], ("dp", "fsdp"), axis=0, tiled=True),
        lax.all_gather(feed_low[3], ("dp", "fsdp"), axis=0, tiled=True),
        lax.all_gather(feed_low[4], ("dp", "fsdp"), axis=0, tiled=True),
        lax.all_gather(feed_low[5], ("dp", "fsdp"), axis=0, tiled=True),
    )
    back_gain_two, back_shift_two, back_up, back_up_shift, back_down, back_down_shift = feed_pieces(
        feed_again
    )
    out_grad = cotangent.astype(jnp.float32)
    grad_down_bias = jnp.sum(out_grad, axis=0)
    grad_down_weight = product_rows(activated, cotangent)
    lifted_back = product_back(cotangent, back_down)
    _, gelu_pull = jax.vjp(jax.nn.gelu, lifted)
    lifted_grad = gelu_pull(lifted_back)[0].astype(jnp.bfloat16)
    grad_up_bias = jnp.sum(lifted_grad.astype(jnp.float32), axis=0)
    grad_up_weight = product_rows(second, lifted_grad)
    second_grad = product_back(lifted_grad, back_up)
    _, norm_pull_two = jax.vjp(normalize, middle, back_gain_two, back_shift_two)
    middle_part, grad_norm2_gain, grad_norm2_bias = norm_pull_two(second_grad)
    middle_grad = out_grad + middle_part
    feed_sums = (
        lax.psum_scatter(grad_norm2_gain, ("dp", "fsdp"), scatter_dimension=0, tiled=True),
        lax.psum_scatter(grad_norm2_bias, ("dp", "fsdp"), scatter_dimension=0, tiled=True),
        lax.psum_scatter(
            grad_up_weight.reshape(-1), ("dp", "fsdp"), scatter_dimension=0, tiled=True
        ),
        lax.psum_scatter(grad_up_bias, ("dp", "fsdp"), scatter_dimension=0, tiled=True),
        lax.psum_scatter(
            grad_down_weight.reshape(-1), ("dp", "fsdp"), scatter_dimension=0, tiled=True
        ),
        lax.psum_scatter(grad_down_bias, ("dp", "fsdp"), scatter_dimension=0, tiled=True),
    )
    attn_again = (
        lax.all_gather(attn_low[0], ("dp", "fsdp"), axis=0, tiled=True),
        lax.all_gather(attn_low[1], ("dp", "fsdp"), axis=0, tiled=True),
        lax.all_gather(attn_low[2], ("dp", "fsdp"), axis=0, tiled=True),
        lax.all_gather(attn_low[3], ("dp", "fsdp"), axis=0, tiled=True),
        lax.all_gather(attn_low[4], ("dp", "fsdp"), axis=0, tiled=True),
        lax.all_gather(attn_low[5], ("dp", "fsdp"), axis=0, tiled=True),
    )
    back_gain_one, back_shift_one, back_qkv, back_pair, back_proj, back_proj_shift = (
        attention_pieces(attn_again)
    )
    branch_grad = middle_grad.astype(jnp.bfloat16)
    grad_out_bias = jnp.sum(branch_grad.astype(jnp.float32), axis=0)
    grad_out_weight = product_rows(context, branch_grad)
    context_grad = product_back(branch_grad, back_proj).reshape(seqs_here, FRAMES, HEADS, HEAD_DIM)
    _, attend_pull = jax.vjp(
        lambda left, middle_in, right: attend(left, middle_in, right, frames),
        queries,
        keys_in,
        values_in,
    )
    query_grad, key_grad, value_grad = attend_pull(context_grad)
    packed_grad = (
        jnp.stack([query_grad, key_grad, value_grad], axis=2)
        .reshape(count, 3 * D)
        .astype(jnp.bfloat16)
    )
    packed_wide = packed_grad.astype(jnp.float32)
    grad_qv_bias = jnp.concatenate(
        [jnp.sum(packed_wide[:, :D], axis=0), jnp.sum(packed_wide[:, 2 * D :], axis=0)]
    )
    grad_qkv_weight = product_rows(first, packed_grad)
    first_grad = product_back(packed_grad, back_qkv)
    _, norm_pull_one = jax.vjp(normalize, states, back_gain_one, back_shift_one)
    states_part, grad_norm1_gain, grad_norm1_bias = norm_pull_one(first_grad)
    tokens_grad = (middle_grad + states_part).astype(jnp.bfloat16)
    attn_sums = (
        lax.psum_scatter(grad_norm1_gain, ("dp", "fsdp"), scatter_dimension=0, tiled=True),
        lax.psum_scatter(grad_norm1_bias, ("dp", "fsdp"), scatter_dimension=0, tiled=True),
        lax.psum_scatter(
            grad_qkv_weight.reshape(-1), ("dp", "fsdp"), scatter_dimension=0, tiled=True
        ),
        lax.psum_scatter(grad_qv_bias, ("dp", "fsdp"), scatter_dimension=0, tiled=True),
        lax.psum_scatter(
            grad_out_weight.reshape(-1), ("dp", "fsdp"), scatter_dimension=0, tiled=True
        ),
        lax.psum_scatter(grad_out_bias, ("dp", "fsdp"), scatter_dimension=0, tiled=True),
    )
    return (
        mixed,
        tokens_grad,
        attn_sums[0],
        attn_sums[1],
        attn_sums[2],
        attn_sums[3],
        attn_sums[4],
        attn_sums[5],
        feed_sums[0],
        feed_sums[1],
        feed_sums[2],
        feed_sums[3],
        feed_sums[4],
        feed_sums[5],
    )


def solution(mesh):
    return jax.shard_map(
        local,
        mesh=mesh,
        in_specs=(
            P(("dp", "fsdp"), None),
            P(("dp", "fsdp")),
            P(("dp", "fsdp")),
            P(("dp", "fsdp")),
            P(("dp", "fsdp")),
            P(("dp", "fsdp")),
            P(("dp", "fsdp")),
            P(("dp", "fsdp")),
            P(("dp", "fsdp")),
            P(("dp", "fsdp")),
            P(("dp", "fsdp")),
            P(("dp", "fsdp")),
            P(("dp", "fsdp")),
            P(("dp", "fsdp")),
            P(("dp", "fsdp"), None),
        ),
        out_specs=(
            P(("dp", "fsdp"), None),
            P(("dp", "fsdp"), None),
            P(("dp", "fsdp")),
            P(("dp", "fsdp")),
            P(("dp", "fsdp")),
            P(("dp", "fsdp")),
            P(("dp", "fsdp")),
            P(("dp", "fsdp")),
            P(("dp", "fsdp")),
            P(("dp", "fsdp")),
            P(("dp", "fsdp")),
            P(("dp", "fsdp")),
            P(("dp", "fsdp")),
            P(("dp", "fsdp")),
        ),
        check_vma=False,
    )
```

profile of v0, /device:TPU:0, one launch (start us, length us, event | category | flops | bytes accessed | tf_op | source)
XLA Modules:
  0.0 594.6 jit_solution(6860326305253836650)
XLA Ops:
  13.0 72.9 %all_gather.46 = bf16[262144]{0:T(1024)(128)(2,1)S(1)} all-gather(bf16[8192]{0:T(1024)(128)(2,1)S(1)} %convert_element_type.142), channel_id=1, replica_groups=mesh['dp'=4,'fsdp'=8] {'dp','fsdp'}, dimensions={0}, use_global_device_ids=true | all-gather | bytes 540672 | tf_op jit(solution)/shard_map/all_gather | solution.py:115
  90.6 37.8 %all-reduce.22 = (bf16[1024]{0:T(1024)(128)(2,1)S(1)}, bf16[512]{0:T(512)(128)(2,1)S(1)}, bf16[512]{0:T(512)(128)(2,1)S(1)}, bf16[512]{0:T(512)(128)(2,1)S(1)}, ...) all-reduce(bf16[1024]{0:T(1024)(128)(2,1)S(1)} %dynamic-update-slic, ...), channel_id=1, replica_groups=mesh['dp'=4,'fsdp'=8] {'dp','fsdp'}, use_global_device_ids=true, to_apply=%add.2 | all-reduce | flops 6144 | bytes 24576
  128.9 3.3 reshape.194
  132.2 3.5 add_convert_fusion
  135.8 8.2 %reshape.195 = bf16[192,5,3,8,64]{4,3,2,1,0:T(8,128)(2,1)} reshape(bf16[960,1536]{1,0:T(8,128)(2,1)} %add_convert_fusion) | data formatting | bytes 5898240 | tf_op jit(solution)/shard_map/reshape | solution.py:124
  143.9 3.8 fusion.55
  150.6 4.1 fusion.49
  154.7 8.1 %convert_bitcast_fusion = bf16[192,5,8,64]{3,1,2,0:T(8,128)(2,1)S(1)} fusion(bf16[192,5,1,8,64]{4,3,2,1,0:T(8,128)(2,1)S(1)} %get-tuple-element.53, f32[192,8,5]{2,1,0:T(8,128)S(1)} %fusion.49, f32[192,8,5,5]{2,3,1,0:T(8,128)S(1)} %get-tuple-element.60, f32[192,8,5]{2,1,0:T(8,128)S(1)} %get-tuple-element.59, pred[192,5,5]{1,2,0:T(8,128)(4,1)S(1)} %broadcast_and_fusion), kind=kOutput, calls=%fused_computation.33 | convolution fusion | flops 30136320 | bytes 2185920 | tf_op jit(solution)/shard_map/shtu,suhe->sthe/dot_general | solution.py:37
  169.0 4.2 reshape.197
  173.2 4.0 fusion.48
  180.3 5.0 convolution_bitcast_fusion.1
  188.0 4.4 reshape.198
  192.4 9.9 %convert_reduce_fusion = (f32[2048]{0:T(1024)S(1)}, bf16[960,2048]{1,0:T(8,128)(2,1)S(1)}) fusion(f32[960,2048]{1,0:T(8,128)} %copy-done.39, f32[2048]{0:T(1024)S(1)} %convert_element_type.152, bf16[960,512]{1,0:T(8,128)(2,1)} %param.29, bf16[2048,512]{1,0:T(8,128)(2,1)} %reshape.198), kind=kOutput, calls=%fused_computation.10 | convolution fusion | flops 2058483712 | bytes 14893056 | tf_op jit(solution)/shard_map/dot_general | solution.py:45
  205.0 4.7 convolution_bitcast_fusion.2
  218.0 3.9 convolution_bitcast_fusion.3
  221.9 6.3 %copy.53 = f32[192,8,64,5]{2,3,1,0:T(8,128)} copy(f32[192,8,64,5]{0,2,1,3:T(8,128)} %convolution_bitcast_fusion.3) | data formatting | bytes 3932160 | tf_op jit(solution)/shard_map/transpose(jvp(shtu,suhe->sthe))/transpose | solution.py:37
  228.2 18.5 %convolution_bitcast_fusion = bf16[192,5,1,8,64]{4,1,3,0,2:T(8,128)(2,1)} fusion(f32[192,8,64,5]{2,3,1,0:T(8,128)} %copy.53, f32[192,8,5]{2,1,0:T(8,128)} %copy-done.6, f32[192,8,5,5]{2,3,1,0:T(8,128)} %copy-done.1, f32[192,8,5]{2,1,0:T(8,128)} %copy-done.14, pred[192,5,5]{1,2,0:T(8,128)(4,1)S(1)} %copy-done.22), kind=kOutput, calls=%fused_computation.50 | convolution fusion | flops 29644800 | bytes 3168960 | tf_op jit(solution)/shard_map/transpose(jvp(shtu,suhe->sthe))/dot_general | solution.py:37
  246.7 17.6 %convert_reduce_fusion.1 = (f32[192,8,5]{2,1,0:T(8,128)}, pred[192,8,5,5]{2,3,1,0:T(8,128)(4,1)}, f32[192,8,5]{2,1,0:T(8,128)}, f32[192,8,5,5]{2,3,1,0:T(8,128)}) fusion(f32[192,8,5]{2,1,0:T(8,128)S(1)} %copy-done.15, f32[192,8,5,5]{2,3,1,0:T(8,128)} %copy-done.1, pred[192,5,5]{1,2,0:T(8,128)(4,1)S(1)} %copy-done.22, f32[192,8,5]{2,1,0:T(8,128)} %multiply_divide_fusion, ...), kind=kOutput, calls=%fused_computation.13 | convolution fusion | flops 29821440 | bytes 3422400 | tf_op jit(solution)/shard_map/transpose(jvp(shtu,suhe->sthe))/dot_general | solution.py:37
  265.5 8.5 %fusion.52 = (f32[192,8,5]{2,1,0:T(8,128)S(1)}, f32[192,8,5,5]{2,3,1,0:T(8,128)}) fusion(f32[192,8,5]{2,1,0:T(8,128)} %copy-done.14, f32[192,8,5,5]{2,3,1,0:T(8,128)S(1)} %bitcast.74, pred[192,5,5]{1,2,0:T(8,128)(4,1)S(1)} %copy-done.22, f32[192,8,5]{2,1,0:T(8,128)S(1)} %neg.16, f32[192,8,5,5]{2,3,1,0:T(8,128)} %get-tuple-element.64, ...), kind=kLoop, calls=%fused_computation.102 | loop fusion | flops 261120 | bytes 588480 | tf_op jit(solution)/shard_map/transpose(jvp())/reduce_sum | solution.py:35
  274.2 12.0 %fusion.27 = bf16[192,5,1,8,64]{4,1,3,0,2:T(8,128)(2,1)} fusion(bf16[192,5,1,8,64]{4,3,2,1,0:T(8,128)(2,1)} %copy-done.19, f32[192,8,5,5]{2,3,1,0:T(8,128)} %get-tuple-element.46, pred[192,8,5,5]{2,3,1,0:T(8,128)(4,1)} %get-tuple-element.48, f32[192,8,5]{2,1,0:T(8,128)S(1)} %negate_divide_fusion, pred[192,5,5]{1,2,0:T(8,128)(4,1)S(1)} %copy-done.22), kind=kOutput, calls=%fused_computation.49 | convolution fusion | flops 29644800 | bytes 2193600 | tf_op jit(solution)/shard_map/transpose(jvp(sthe,suhe->shtu))/dot_general | solution.py:28
  286.1 10.2 %fusion.26 = bf16[192,5,1,8,64]{4,1,3,0,2:T(8,128)(2,1)} fusion(bf16[192,5,1,8,64]{4,3,2,1,0:T(8,128)(2,1)S(1)} %copy-done.18, f32[192,8,5,5]{2,3,1,0:T(8,128)} %get-tuple-element.46, pred[192,8,5,5]{2,3,1,0:T(8,128)(4,1)S(1)} %copy-done.40, f32[192,8,5]{2,1,0:T(8,128)S(1)} %negate_divide_fusion, pred[192,5,5]{1,2,0:T(8,128)(4,1)S(1)} %copy-done.22), kind=kOutput, calls=%fused_computation.48 | convolution fusion | flops 29644800 | bytes 2193600 | tf_op jit(solution)/shard_map/transpose(jvp(sthe,suhe->shtu))/dot_general | solution.py:28
  303.6 4.9 copy.58
  308.5 4.7 copy.56
  313.2 4.7 copy.57
  317.9 3.9 maximum_convert_fusion
  321.8 9.9 %copy.59 = bf16[192,5,3,8,64]{4,3,2,1,0:T(8,128)(2,1)} copy(bf16[192,5,3,8,64]{0,4,3,2,1:T(8,128)(2,1)} %maximum_convert_fusion) | data formatting | bytes 5898240 | tf_op jit(solution)/shard_map/convert_element_type | solution.py:203
  331.7 8.3 %convert_element_type.163 = bf16[960,1536]{1,0:T(8,128)(2,1)} reshape(bf16[192,5,3,8,64]{4,3,2,1,0:T(8,128)(2,1)} %copy.59) | data formatting | bytes 5898240 | tf_op jit(solution)/shard_map/convert_element_type | solution.py:203
  340.0 5.4 fusion.44
  345.4 4.4 reshape.199
  360.1 40.7 %all-reduce.20 = (f32[512]{0:T(512)S(1)}, f32[512]{0:T(512)S(1)}, f32[1024]{0:T(1024)S(1)}, f32[512]{0:T(512)S(1)}, f32[512]{0:T(512)S(1)}, /*index=5*/f32[512]{0:T(512)S(1)}, f32[2048]{0:T(1024)S(1)}, f32[512]{0:T(512)S(1)}) all-reduce(f32[512]{0:T(512)S(1)} %get-tuple-element.18, ...), channel_id=2, replica_groups=mesh['dp'=4,'fsdp'=8] {'dp','fsdp'}, use_global_device_ids=true, to_apply=%region_14.15.clone | all-reduce | flops 6144 | bytes 49152
  405.5 7.9 %add_convert_fusion.2 = bf16[960,512]{1,0:T(8,128)(2,1)} fusion(f32[960,512]{1,0:T(8,128)S(1)} %get-tuple-element.62, bf16[2048,512]{1,0:T(8,128)(2,1)} %reshape.198, f32[512]{0:T(512)S(1)} %convert_element_type.156, f32[960,2048]{1,0:T(8,128)} %copy-done.39, f32[2048]{0:T(1024)S(1)} %convert_element_type.152), kind=kOutput, calls=%fused_computation.69 | convolution fusion | flops 2034401280 | bytes 12920832 | tf_op jit(solution)/shard_map/dot_general | solution.py:41
  413.4 168.4 %all-reduce.25.cloned.1.call-done = (f32[786432]{0:T(1024)}, f32[262144]{0:T(1024)}, f32[1048576]{0:T(1024)}, f32[1048576]{0:T(1024)}) async-done(((f32[786432]{0:T(1024)}, f32[262144]{0:T(1024)}, f32[1048576]{0:T(1024)}, f32[1048576]{0:T(1024)}), (f32[786432]{0:T(1024)}, f32[262144]{0:T(1024)}, f32[1048576]{0:T(1024)}, f32[1048576]{0:T(1024)})) %all-reduce.25.cloned.1.call-update) | async-done | bytes 12582928
  (185 shorter events, 66.0 us)
Async XLA Ops:
  7.2 80.2 %copy-start.31 = (f32[16]{0:T(128)S(1)}, f32[16]{0:T(128)}, u32[]{:S(2)}) copy-start(f32[16]{0:T(128)} %param.17) | copy-start | bytes 196
  7.2 80.2 %copy-start.32 = (f32[16]{0:T(128)S(1)}, f32[16]{0:T(128)}, u32[]{:S(2)}) copy-start(f32[16]{0:T(128)} %param.18) | copy-start | bytes 196
  7.2 80.2 %copy-start.33 = (f32[32]{0:T(128)S(1)}, f32[32]{0:T(128)}, u32[]{:S(2)}) copy-start(f32[32]{0:T(128)} %param.20) | copy-start | bytes 388
  7.2 80.2 %copy-start.34 = (f32[16]{0:T(128)S(1)}, f32[16]{0:T(128)}, u32[]{:S(2)}) copy-start(f32[16]{0:T(128)} %param.22) | copy-start | bytes 196
  7.2 80.2 %copy-start.35 = (f32[16]{0:T(128)S(1)}, f32[16]{0:T(128)}, u32[]{:S(2)}) copy-start(f32[16]{0:T(128)} %param.23) | copy-start | bytes 196
  7.2 80.2 %copy-start.36 = (f32[16]{0:T(128)S(1)}, f32[16]{0:T(128)}, u32[]{:S(2)}) copy-start(f32[16]{0:T(128)} %param.24) | copy-start | bytes 196
  7.2 80.2 %copy-start.37 = (f32[64]{0:T(128)S(1)}, f32[64]{0:T(128)}, u32[]{:S(2)}) copy-start(f32[64]{0:T(128)} %param.26) | copy-start | bytes 772
  7.3 80.2 %copy-start.38 = (f32[16]{0:T(128)S(1)}, f32[16]{0:T(128)}, u32[]{:S(2)}) copy-start(f32[16]{0:T(128)} %param.28) | copy-start | bytes 196
  7.3 80.2 %copy-start.2 = (bf16[960,512]{1,0:T(8,128)(2,1)S(1)}, bf16[960,512]{1,0:T(8,128)(2,1)}, u32[]{:S(2)}) copy-start(bf16[960,512]{1,0:T(8,128)(2,1)} %param.15) | copy-start | bytes 2949124
  7.3 121.2 %copy-start.30 = (s32[192]{0:T(256)S(1)}, s32[192]{0:T(256)}, u32[]{:S(2)}) copy-start(s32[192]{0:T(256)} %param.16) | copy-start | bytes 2308
  7.3 121.6 %all-gather.4.cloned.1.call-start = ((), (), s32[]{:S(2)}) async-start(), calls=%async_computation | async-start | bytes 1622016 | tf_op jit(solution)/shard_map/all_gather | solution.py:113
  9.0 160.0 %all-gather.6.cloned.1.call-start = ((), (), s32[]{:S(2)}) async-start(), calls=%async_computation.1 | async-start | bytes 2162688 | tf_op jit(solution)/shard_map/all_gather | solution.py:133
  10.6 177.5 %all-gather.8.cloned.1.call-start = ((), (), s32[]{:S(2)}) async-start(), calls=%async_computation.2 | async-start | bytes 2162688 | tf_op jit(solution)/shard_map/all_gather | solution.py:135
  12.2 569.6 %all-reduce.25.cloned.1.call-start = ((), (), s32[]{:S(2)}) async-start(), calls=%async_computation.3 | async-start | bytes 25165824
  128.8 25.9 %copy-start.21 = (pred[192,5,5]{1,2,0:T(8,128)(4,1)}, pred[192,5,5]{1,2,0:T(8,128)(4,1)S(1)}, u32[]{:S(2)}) copy-start(pred[192,5,5]{1,2,0:T(8,128)(4,1)S(1)} %broadcast_and_fusion) | copy-start | bytes 14404
  132.2 3.6 copy-start.23
  147.7 7.0 %copy-start.20 = (bf16[192,5,1,8,64]{4,3,2,1,0:T(8,128)(2,1)}, bf16[192,5,1,8,64]{4,3,2,1,0:T(8,128)(2,1)S(1)}, u32[]{:S(2)}) copy-start(bf16[192,5,1,8,64]{4,3,2,1,0:T(8,128)(2,1)S(1)} %get-tuple-element.53) | copy-start | bytes 2949124
  150.6 4.1 copy-start.1
  150.6 4.1 copy-start.14
  154.7 8.2 %copy-start.6 = (f32[192,8,5]{2,1,0:T(8,128)}, f32[192,8,5]{2,1,0:T(8,128)S(1)}, u32[]{:S(2)}) copy-start(f32[192,8,5]{2,1,0:T(8,128)S(1)} %fusion.49) | copy-start | bytes 92164
  173.2 7.1 %copy-start.10 = (bf16[960,512]{1,0:T(8,128)(2,1)S(1)}, bf16[960,512]{1,0:T(8,128)(2,1)}, u32[]{:S(2)}) copy-start(bf16[960,512]{1,0:T(8,128)(2,1)} %param.29) | copy-start | bytes 2949124
  177.1 3.2 copy-start.39
  192.4 9.9 %copy-start.16 = (bf16[512,2048]{1,0:T(8,128)(2,1)S(1)}, bf16[512,2048]{1,0:T(8,128)(2,1)}, u32[]{:S(2)}) copy-start(bf16[512,2048]{1,0:T(8,128)(2,1)} %reshape.197) | copy-start | bytes 6291460
  221.9 6.3 %copy-start.22 = (pred[192,5,5]{1,2,0:T(8,128)(4,1)S(1)}, pred[192,5,5]{1,2,0:T(8,128)(4,1)}, u32[]{:S(2)}) copy-start(pred[192,5,5]{1,2,0:T(8,128)(4,1)} %copy-done.21) | copy-start | bytes 14404
  228.2 18.5 %copy-start.15 = (f32[192,8,5]{2,1,0:T(8,128)S(1)}, f32[192,8,5]{2,1,0:T(8,128)}, u32[]{:S(2)}) copy-start(f32[192,8,5]{2,1,0:T(8,128)} %copy-done.14) | copy-start | bytes 92164
  228.2 37.3 %slice-start = ((s8[6291456]{0:T(1024)(128)(4,1)}), s8[4194304]{0:T(1024)(128)(4,1)S(1)}, s32[]{:S(2)}) async-start(s8[6291456]{0:T(1024)(128)(4,1)} %bitcast.73), calls=%async_computation.4 | async-start | bytes 8388608
  246.7 18.8 %slice-start.1 = ((s8[6291456]{0:T(1024)(128)(4,1)}), s8[2097152]{0:T(1024)(128)(4,1)S(1)}, s32[]{:S(2)}) async-start(s8[6291456]{0:T(1024)(128)(4,1)} %bitcast.73), calls=%async_computation.5 | async-start | bytes 4194304
  246.7 18.8 %copy-start.8 = (f32[192,8,5]{2,1,0:T(8,128)S(1)}, f32[192,8,5]{2,1,0:T(8,128)}, u32[]{:S(2)}) copy-start(f32[192,8,5]{2,1,0:T(8,128)} %copy-done.6) | copy-start | bytes 92164
  265.5 8.5 %copy-start.27 = (f32[192,8,5]{2,1,0:T(8,128)S(1)}, f32[192,8,5]{2,1,0:T(8,128)}, u32[]{:S(2)}) copy-start(f32[192,8,5]{2,1,0:T(8,128)} %get-tuple-element.47) | copy-start | bytes 92164
  274.1 12.0 %copy-start.18 = (bf16[192,5,1,8,64]{4,3,2,1,0:T(8,128)(2,1)S(1)}, bf16[192,5,1,8,64]{4,3,2,1,0:T(8,128)(2,1)}, u32[]{:S(2)}) copy-start(bf16[192,5,1,8,64]{4,3,2,1,0:T(8,128)(2,1)} %copy-done.17) | copy-start | bytes 2949124
  274.2 12.0 %copy-start.40 = (pred[192,8,5,5]{2,3,1,0:T(8,128)(4,1)S(1)}, pred[192,8,5,5]{2,3,1,0:T(8,128)(4,1)}, u32[]{:S(2)}) copy-start(pred[192,8,5,5]{2,3,1,0:T(8,128)(4,1)} %get-tuple-element.48) | copy-start | bytes 115204
  286.1 10.2 %copy-start.9 = (f32[256,4,8,128]{3,2,1,0:T(8,128)S(1)}, f32[256,4,8,128]{3,2,1,0:T(8,128)}, u32[]{:S(2)}) copy-start(f32[256,4,8,128]{3,2,1,0:T(8,128)} %convolution_bitcast_fusion.1) | copy-start | bytes 12582916
  (15 other events, 32.4 us)
Sparse Core Ops, SparseCore 0:
  11.6 58.0 all-gather.3
  73.2 55.7 all-gather.5
  132.5 55.4 all-gather.7
  349.9 231.7 all-reduce.24
where the time goes:
time: 600 us; the launch traced here: 595 us
  waiting for transfers between devices  171 us (28%)
  blocking collectives  151 us (25%)
  matrix products  122 us (20%)
  local copies, waits for them, and re-layouts  102 us (17%)
  other arithmetic  32.9 us (5%)
  between operations  14.8 us (2%)
    unnamed x5, waiting for transfers between devices  168 us
    unnamed x2, blocking collectives  78.4 us
    all_gather x1, blocking collectives, local(): lax.all_gather(attn_low[4], ('dp', 'fsdp'), axis=0, tiled=True)  72.9 us
    dot_general x3, matrix products, attend(): return jnp.einsum('shtu,suhe->sthe', weights, values_in, precision=PRECISE)  44.2 us
    unnamed x117, local copies, waits for them, and re-layouts  28.2 us
    dot_general x3, matrix products, attend(): jnp.einsum('sthe,suhe->shtu', queries, keys_in, precision=PRECISE) * scale  25 us
    dot_general x4, matrix products, product_back(): lax.dot_general(left, right, (((1,), (1,)), ((), ())), preferred_element_...  18.4 us
    convert_element_type x2, local copies, waits for them, and re-layouts, local(): packed_grad = jnp.stack([query_grad, key_grad, value_grad], axis=2).resha...  18.1 us
  transfers between devices with their start and end apart: 4, of which 2 were waited for; matrix products, arithmetic and copies ran while one was open for 14% of the time, Pallas kernels for 0%

commit v1 on v0

v1 whole, which is shorter than its diff:
```python
import math

import jax
import jax.numpy as jnp
from jax import lax
from jax.experimental import pallas as pl
from jax.experimental.pallas import tpu as pltpu
from jax.sharding import PartitionSpec as P

D = 512
HEADS = 8
HEAD_DIM = 64
FF = 2048
FRAMES = 5
EPSILON = 1e-05
PAIRS = [(t, u) for t in range(FRAMES) for u in range(t + 1)]

F32 = jnp.float32
BF16 = jnp.bfloat16
MESH = pl.DeviceIdType.MESH

SM, QKV, OUT, UP, DOWN = range(5)
ROWS = (8, 16, 16, 16, 64)
COLS = (128, 3 * D, D, FF, D)
KEPT = (F32, BF16, BF16, BF16, BF16)
SMALL = (16, 16, 32, 16, 16, 16, 64, 16)
GAIN1, BIAS1, QVB, OUTB, GAIN2, BIAS2, UPB, DOWNB = range(8)

TILE = 64
CHUNK = 32


def dot(left, right):
    return lax.dot_general(left, right, (((1,), (0,)), ((), ())), preferred_element_type=F32)


def dot_nt(left, right):
    return lax.dot_general(left, right, (((1,), (1,)), ((), ())), preferred_element_type=F32)


def dot_tn(left, right):
    return lax.dot_general(left, right, (((0,), (0,)), ((), ())), preferred_element_type=F32)


def iota(shape, dim):
    return lax.broadcasted_iota(jnp.int32, shape, dim)


def fold(values):
    rows, cols = values.shape
    return jnp.sum(values.reshape(rows // 8, 8, cols), axis=0)


def split_two(values):
    high = values.astype(BF16)
    return high, (values - high.astype(F32)).astype(BF16)


def layer_kernel(split, count, *refs):
    refs = list(refs)

    def take(n):
        head = refs[:n]
        del refs[:n]
        return head

    tok_hbm, cot_hbm, frames_ref = take(3)
    small_in = take(8)
    shard_in = [None] + take(4)
    mixed_hbm, tgrad_hbm = take(2)
    small_out = take(8)
    shard_out = [None] + take(4)
    whole = take(5)
    acc = take(5)
    sib_out, sib_in = take(5), take(5)
    two_out, two_in = take(5), take(5)
    one_out, one_in = take(5), take(5)
    zed_out, zed_in = take(5), take(5)
    (tokb, cotb, stage, xt, dm, xh1, xh2, rs1, rs2, a1, a2, qkv, prob, ctx, x1, act, slope, wide, dao, dpre) = take(20)
    (vec16, vecqv, vecup, biasq, living, pick, pick_t, gs16, gsqv, gsup, sums) = take(11)
    (gsend, grecv, rsend, rrecv, io_sem) = take(5)

    seqs = count // FRAMES
    dp = lax.axis_index("dp")
    fs = lax.axis_index("fsdp")
    x, c = dp // 2, dp % 2
    group, rest = fs // split, fs % split
    z, y = group // 2, group % 2

    def device(x_, c_, z_, y_):
        return (x_ * 2 + c_, (z_ * 2 + y_) * split + rest)

    first = x + c * (y - x)
    second = y + c * (x - y)

    def to_xy(f_, s_):
        return f_ + c * (s_ - f_), s_ + c * (f_ - s_)

    def peer(f_, s_):
        x_, y_ = to_xy(f_, s_)
        return device(x_, c, z, y_)

    sibling = device(x, 1 - c, z, y)
    first_dev = peer(1 - first, second)
    second_dev = peer(first, 1 - second)
    zeds = (z + 1 - 2 * (z % 2), (z + 2) % 4, 3 - z)
    zed_dev = [device(x, c, zk, y) for zk in zeds]

    tok_copy = pltpu.make_async_copy(tok_hbm, tokb, io_sem.at[0])
    cot_copy = pltpu.make_async_copy(cot_hbm, cotb, io_sem.at[1])
    tok_copy.start()
    cot_copy.start()
    barrier = pltpu.get_barrier_semaphore()
    for dev in [sibling, first_dev, second_dev] + zed_dev:
        pl.semaphore_signal(barrier, inc=1, device_id=dev, device_id_type=MESH)

    def shard(w, f_, s_, z_):
        x_, y_ = to_xy(f_, s_)
        return whole[w].at[x_, c, z_, y_]

    def line(w, f_, s_):
        x_, y_ = to_xy(f_, s_)
        return whole[w].at[x_, c, :, y_]

    def gcopy(w, k, ref, dev):
        return pltpu.make_async_remote_copy(
            src_ref=ref, dst_ref=ref, send_sem=gsend.at[w, k], recv_sem=grecv.at[w, k], device_id=dev, device_id_type=MESH
        )

    def own_shard(w):
        if w == SM:
            whole[w][x, c, z, y] = jnp.zeros((8, 128), F32)
            for p, n in enumerate(SMALL):
                whole[w][x, c, z, y, p : p + 1, 0:n] = small_in[p][...].astype(BF16).astype(F32)
        else:
            step = COLS[w] // 128
            for k in range(step):
                part = shard_in[w][pl.ds(k, ROWS[w], stride=step), :]
                whole[w][x, c, z, y, :, k * 128 : (k + 1) * 128] = part.astype(BF16)

    def g_start(w):
        ref = shard(w, first, second, z)
        for k in range(3):
            gcopy(w, k, ref, zed_dev[k]).start()
        gcopy(w, 3 + z, ref, first_dev).start()
        gcopy(w, 7 + z, ref, second_dev).start()

    def g_z(w):
        for k in range(3):
            ref = shard(w, first, second, zeds[k])
            gcopy(w, k, ref, zed_dev[k]).wait_recv()
            gcopy(w, 3 + zeds[k], ref, first_dev).start()
            gcopy(w, 7 + zeds[k], ref, second_dev).start()
        gcopy(w, 15, line(w, first, second), sibling).start()

    def g_f(w):
        for k in range(4):
            ref = shard(w, 1 - first, second, k)
            gcopy(w, 3 + k, ref, first_dev).wait_recv()
            gcopy(w, 11 + k, ref, second_dev).start()
        gcopy(w, 16, line(w, 1 - first, second), sibling).start()

    def g_s(w):
        for k in range(4):
            gcopy(w, 7 + k, shard(w, first, 1 - second, k), second_dev).wait_recv()
        gcopy(w, 17, line(w, first, 1 - second), sibling).start()
        for k in range(4):
            gcopy(w, 11 + k, shard(w, 1 - first, 1 - second, k), second_dev).wait_recv()
        gcopy(w, 18, line(w, 1 - first, 1 - second), sibling).start()

    def g_sib(w):
        for k, (flip_f, flip_s) in enumerate(((0, 0), (0, 1), (1, 0), (1, 1))):
            x_, y_ = to_xy(first + flip_f * (1 - 2 * first), second + flip_s * (1 - 2 * second))
            gcopy(w, 15 + k, whole[w].at[x_, 1 - c, :, y_], sibling).wait_recv()

    def g_end(w):
        own = shard(w, first, second, z)
        for k in range(15):
            gcopy(w, k, own, sibling).wait_send()
        for k in range(15, 19):
            gcopy(w, k, line(w, first, second), sibling).wait_send()

    def place(f_, s_, z_):
        x_, y_ = to_xy(f_, s_)
        return x_ * 8 + z_ * 2 + y_

    def rcopy(w, k, src, dst, dev):
        return pltpu.make_async_remote_copy(
            src_ref=src, dst_ref=dst, send_sem=rsend.at[w, k], recv_sem=rrecv.at[w, k], device_id=dev, device_id_type=MESH
        )

    def sib_copy(w, h):
        return rcopy(w, h, sib_out[w].at[pl.ds(8 * h, 8)], sib_in[w].at[pl.ds(8 * h, 8)], sibling)

    def two_copy(w, k):
        return rcopy(w, 2 + k, two_out[w].at[k], two_in[w].at[k], second_dev)

    def one_copy(w, k):
        return rcopy(w, 10 + k, one_out[w].at[k], one_in[w].at[k], first_dev)

    def zed_copy(w, k):
        return rcopy(w, 14 + k, zed_out[w].at[k], zed_in[w].at[k], zed_dev[k])

    def r_1(w):
        for h in range(2):
            sib_copy(w, h).wait_recv()

        def step(k, carry):
            j = place(k // 4, 1 - second, k % 4)
            two_out[w][k] = (acc[w][j] + sib_in[w][j].astype(F32)).astype(KEPT[w])
            two_copy(w, k).start()
            return carry

        lax.fori_loop(0, 8, step, 0)

    def r_2(w):
        def step(k, carry):
            j = place(1 - first, second, k)
            slot = (1 - first) * 4 + k
            two_copy(w, slot).wait_recv()
            total = acc[w][j] + sib_in[w][j].astype(F32) + two_in[w][slot].astype(F32)
            one_out[w][k] = total.astype(KEPT[w])
            one_copy(w, k).start()
            return carry

        lax.fori_loop(0, 4, step, 0)

    def r_3(w):
        for k in range(3):
            j = place(first, second, zeds[k])
            slot = first * 4 + zeds[k]
            two_copy(w, slot).wait_recv()
            one_copy(w, zeds[k]).wait_recv()
            total = acc[w][j] + sib_in[w][j].astype(F32) + two_in[w][slot].astype(F32) + one_in[w][zeds[k]].astype(F32)
            zed_out[w][k] = total.astype(KEPT[w])
            zed_copy(w, k).start()

    def r_4(w):
        j = place(first, second, z)
        slot = first * 4 + z
        two_copy(w, slot).wait_recv()
        one_copy(w, z).wait_recv()
        total = acc[w][j] + sib_in[w][j].astype(F32) + two_in[w][slot].astype(F32) + one_in[w][z].astype(F32)
        for k in range(3):
            zed_copy(w, k).wait_recv()
            total = total + zed_in[w][k].astype(F32)
        if w == SM:
            for p, n in enumerate(SMALL):
                small_out[p][...] = total[p : p + 1, 0:n]
        else:
            step = COLS[w] // 128
            for k in range(step):
                shard_out[w][pl.ds(k, ROWS[w], stride=step), :] = total[:, k * 128 : (k + 1) * 128]

    def r_end(w):
        for h in range(2):
            sib_copy(w, h).wait_send()
        for k in range(8):
            two_copy(w, k).wait_send()
        for k in range(4):
            one_copy(w, k).wait_send()
        for k in range(3):
            zed_copy(w, k).wait_send()

    tiles = count // TILE
    per_frame = seqs // TILE

    def tile_rows(i):
        return pl.ds(pl.multiple_of(i * TILE, TILE), TILE)

    def strided(i):
        return pl.ds(i // per_frame + FRAMES * TILE * (i % per_frame), TILE, stride=FRAMES)

    def loop(n, body):
        def step(i, carry):
            body(i)
            return carry

        lax.fori_loop(0, n, step, 0)

    def widen(src):
        def body(i):
            for h in range(4):
                stage[h, tile_rows(i), :] = src[tile_rows(i), h * 128 : (h + 1) * 128].astype(F32)

        loop(tiles, body)

    def narrow(dst):
        def body(i):
            for h in range(4):
                dst[tile_rows(i), h * 128 : (h + 1) * 128] = stage[h, tile_rows(i), :].astype(BF16)

        loop(tiles, body)

    def center(values):
        mean = jnp.mean(values, axis=-1, keepdims=True)
        centered = values - mean
        root = lax.rsqrt(jnp.mean(centered * centered, axis=-1, keepdims=True) + EPSILON)
        return centered * root, root

    def constants():
        lane, row = iota((D, 128), 1), iota((D, 128), 0)
        pick[...] = jnp.where((row // HEAD_DIM == lane % HEADS) & (lane < 2 * HEADS), 1.0, 0.0).astype(BF16)
        lane, row = iota((128, D), 1), iota((128, D), 0)
        pick_t[...] = jnp.where((lane // HEAD_DIM == row % HEADS) & (row < 2 * HEADS), 1.0, 0.0).astype(BF16)
        same = iota((seqs, seqs), 0) == iota((seqs, seqs), 1)
        wide_frames = jnp.broadcast_to(frames_ref[...].astype(F32), (seqs, seqs))
        spread = jnp.where(same, wide_frames, 0.0).astype(BF16)
        living[...] = dot(spread, jnp.ones((seqs, 128), BF16))
        gs16[...] = jnp.zeros_like(gs16)
        gsqv[...] = jnp.zeros_like(gsqv)
        gsup[...] = jnp.zeros_like(gsup)

    def first_norm():
        widen(tokb)

        def body(i):
            values = jnp.concatenate([stage[h, strided(i), :] for h in range(4)], axis=1)
            xt[tile_rows(i), :] = values.astype(BF16)
            hat, root = center(values)
            xh1[tile_rows(i), :] = hat
            rs1[tile_rows(i), :] = jnp.broadcast_to(root, (TILE, 128))

        loop(tiles, body)

    def cotangent_in():
        widen(cotb)

        def body(i):
            values = jnp.concatenate([stage[h, strided(i), :] for h in range(4)], axis=1)
            dm[tile_rows(i), :] = values.astype(BF16)
            gs16[DOWNB : DOWNB + 1, :] += jnp.sum(fold(values), axis=0, keepdims=True)

        loop(tiles, body)

    def small_vectors():
        raw = whole[SM][...].reshape(256, 128).astype(BF16)
        for n, dst in ((16, vec16), (32, vecqv), (64, vecup)):
            width = 32 * n
            for at in range(0, width, 512):
                near = iota((128, 512), 0) == (iota((128, 512), 1) + at) % n
                spread = dot(raw, jnp.where(near, 1.0, 0.0).astype(BF16))
                mine = iota((256, 512), 0) // 8 == (iota((256, 512), 1) + at) // n
                dst[:, at : at + 512] = jnp.sum(jnp.where(mine, spread, 0.0).reshape(32, 8, 512), axis=0)
        biasq[:, 0:D] = vecqv[QVB : QVB + 1, 0:D]
        biasq[:, D : 2 * D] = jnp.zeros((1, D), F32)
        biasq[:, 2 * D : 3 * D] = vecqv[QVB : QVB + 1, D : 2 * D]

    def small_grads():
        for n, src in ((16, gs16), (32, gsqv), (64, gsup)):
            width = 32 * n
            for at in range(0, width, 512):
                mine = iota((256, 512), 0) // 8 == (iota((256, 512), 1) + at) // n
                values = jnp.broadcast_to(src[:, at : at + 512][None], (32, 8, 512)).reshape(256, 512)
                high, low = split_two(jnp.where(mine, values, 0.0))
                near = jnp.where(iota((128, 512), 0) == (iota((128, 512), 1) + at) % n, 1.0, 0.0).astype(BF16)
                part = dot_nt(high, near) + dot_nt(low, near)
                total = part if n == 16 and at == 0 else total + part
        sums[...] = total.reshape(2, 2, 8, 8, 128)
        for h in range(2):
            acc[SM][8 * h : 8 * h + 8] = sums[h, c]
            sib_out[SM][8 * h : 8 * h + 8] = sums[h, 1 - c]
            sib_copy(SM, h).start()

    def first_affine():
        gain, bias = vec16[GAIN1 : GAIN1 + 1, :], vec16[BIAS1 : BIAS1 + 1, :]

        def body(i):
            a1[tile_rows(i), :] = (xh1[tile_rows(i), :] * gain + bias).astype(BF16)

        loop(tiles, body)

    def cols(n, width):
        return pl.ds(pl.multiple_of(n * width, width), width)

    def matrix_cols(w, n, width):
        part = whole[w][:, :, :, :, :, cols(n, width)]
        return part.reshape(32 * ROWS[w], width)

    def matrix(w):
        return whole[w][...].reshape(32 * ROWS[w], COLS[w])

    def project_in():
        def body(n):
            r = dot(a1[...], matrix_cols(QKV, n, 256)) + biasq[:, cols(n, 256)]
            qkv[:, cols(n, 256)] = r.astype(BF16)

        loop(6, body)

    def frame_rows(t, i):
        return pl.ds(pl.multiple_of(t * seqs + i * CHUNK, CHUNK), CHUNK)

    def heads_of(i, part):
        return [qkv[frame_rows(t, i), part * D : (part + 1) * D].astype(F32) for t in range(FRAMES)]

    def spread_heads(parts):
        lanes = iota((CHUNK, 128), 1)
        mixed_parts = []
        for part in parts:
            high, low = split_two(part)
            mixed_parts.append(jnp.where(lanes < HEADS, high.astype(F32), low.astype(F32)).astype(BF16))
        return dot(jnp.concatenate(mixed_parts, axis=0), pick_t[...])

    def rows_of(values, k):
        return values[k * CHUNK : (k + 1) * CHUNK]

    def attention(i):
        q, k_, v = heads_of(i, 0), heads_of(i, 1), heads_of(i, 2)
        halves = [split_two(q[t] * k_[u]) for t, u in PAIRS]
        high = jnp.concatenate([h for h, _ in halves], axis=0)
        low = jnp.concatenate([l for _, l in halves], axis=0)
        scores = (dot(high, pick[...]) + dot(low, pick[...])) * (1.0 / math.sqrt(HEAD_DIM))
        live = living[pl.ds(pl.multiple_of(i * CHUNK, CHUNK), CHUNK), :]
        weights = []
        for t in range(FRAMES):
            row = [rows_of(scores, PAIRS.index((t, u))) for u in range(t + 1)]
            row = [jnp.where(u < live, part, -1e30) for u, part in enumerate(row)]
            top = row[0]
            for part in row[1:]:
                top = jnp.maximum(top, part)
            row = [jnp.exp(part - top) for part in row]
            total = row[0]
            for part in row[1:]:
                total = total + part
            weights += [part / total for part in row]
        for k, part in enumerate(weights):
            prob[k, pl.ds(pl.multiple_of(i * CHUNK, CHUNK), CHUNK), :] = part
        spread = spread_heads(weights)
        for t in range(FRAMES):
            total = rows_of(spread, PAIRS.index((t, 0))) * v[0]
            for u in range(1, t + 1):
                total = total + rows_of(spread, PAIRS.index((t, u))) * v[u]
            ctx[frame_rows(t, i), :] = total.astype(BF16)

    def attention_back(i):
        v = heads_of(i, 2)
        g = [wide[frame_rows(t, i), :] for t in range(FRAMES)]
        products = jnp.concatenate([(g[t] * v[u]).astype(BF16) for t, u in PAIRS], axis=0)
        slopes = dot(products, pick[...])
        weights = [prob[k, pl.ds(pl.multiple_of(i * CHUNK, CHUNK), CHUNK), :] for k in range(len(PAIRS))]
        scaled = []
        for t in range(FRAMES):
            ks = [PAIRS.index((t, u)) for u in range(t + 1)]
            mean = weights[ks[0]] * rows_of(slopes, ks[0])
            for k in ks[1:]:
                mean = mean + weights[k] * rows_of(slopes, k)
            scaled += [weights[k] * (rows_of(slopes, k) - mean) * (1.0 / math.sqrt(HEAD_DIM)) for k in ks]
        spread_p = spread_heads(weights)
        for u in range(FRAMES):
            total = None
            for t in range(u, FRAMES):
                part = rows_of(spread_p, PAIRS.index((t, u))) * g[t]
                total = part if total is None else total + part
            low = total.astype(BF16)
            dpre[frame_rows(u, i), 2 * D :] = low
            gsqv[QVB : QVB + 1, D:] += jnp.sum(fold(low.astype(F32)), axis=0, keepdims=True)
        q, k_ = heads_of(i, 0), heads_of(i, 1)
        spread_s = spread_heads(scaled)
        for t in range(FRAMES):
            total = None
            for u in range(t + 1):
                part = rows_of(spread_s, PAIRS.index((t, u))) * k_[u]
                total = part if total is None else total + part
            low = total.astype(BF16)
            dpre[frame_rows(t, i), :D] = low
            gsqv[QVB : QVB + 1, :D] += jnp.sum(fold(low.astype(F32)), axis=0, keepdims=True)
        for u in range(FRAMES):
            total = None
            for t in range(u, FRAMES):
                part = rows_of(spread_s, PAIRS.index((t, u))) * q[t]
                total = part if total is None else total + part
            dpre[frame_rows(u, i), D : 2 * D] = total.astype(BF16)

    def project_out():
        bias = vec16[OUTB : OUTB + 1, :]
        for n in range(2):
            at = slice(n * 256, (n + 1) * 256)
            r = dot(ctx[...], whole[OUT][:, :, :, :, :, at].reshape(D, 256))
            x1[:, at] = xt[:, at].astype(F32) + r + bias[:, at]

    def second_norm():
        gain, bias = vec16[GAIN2 : GAIN2 + 1, :], vec16[BIAS2 : BIAS2 + 1, :]

        def body(i):
            hat, root = center(x1[tile_rows(i), :])
            xh2[tile_rows(i), :] = hat
            rs2[tile_rows(i), :] = jnp.broadcast_to(root, (TILE, 128))
            a2[tile_rows(i), :] = (hat * gain + bias).astype(BF16)

        loop(tiles, body)

    def feed_up():
        k0 = math.sqrt(2.0 / math.pi)
        k1 = k0 * 0.044715

        def body(n):
            f = dot(a2[...], matrix_cols(UP, n, 256)) + vecup[UPB : UPB + 1, cols(n, 256)]
            square = f * f
            half = 0.5 + 0.5 * jnp.tanh(f * (k0 + k1 * square))
            act[:, cols(n, 256)] = (f * half).astype(BF16)
            grow = half + (f * (half - half * half)) * (2.0 * k0 + 6.0 * k1 * square)
            slope[:, cols(n, 256)] = grow.astype(BF16)

        loop(8, body)

    def feed_down():
        bias = vec16[DOWNB : DOWNB + 1, :]
        for n in range(2):
            at = slice(n * 256, (n + 1) * 256)
            r = dot(act[...], whole[DOWN][:, :, :, :, :, at].reshape(FF, 256))
            r = r + x1[:, at] + bias[:, at]
            for t in range(FRAMES):
                stage_rows = pl.ds(t, seqs, stride=FRAMES)
                for h in range(2):
                    stage[2 * n + h, stage_rows, :] = r[t * seqs : (t + 1) * seqs, h * 128 : (h + 1) * 128]
        narrow(tokb)

    def weight_grad(w, left, right, h_rows, width):
        def lhs(core):
            parts = [left[:, pl.ds(pl.multiple_of(h * 2 * h_rows + core * h_rows, 128), h_rows)] for h in range(2)]
            return jnp.concatenate(parts, axis=1)

        def theirs(n):
            r = dot_tn(lhs(1 - c), right[:, cols(n, width)])
            sib_out[w][:, :, cols(n, width)] = r.reshape(16, ROWS[w], width).astype(BF16)

        def ours(n):
            r = dot_tn(lhs(c), right[:, cols(n, width)])
            acc[w][:, :, cols(n, width)] = r.reshape(16, ROWS[w], width)

        loop(COLS[w] // width, theirs)
        for h in range(2):
            sib_copy(w, h).start()
        loop(COLS[w] // width, ours)

    def down_grad():
        def theirs(h):
            left = act[:, pl.ds(pl.multiple_of(h * 1024 + (1 - c) * 512, 512), 512)]
            r = dot_tn(left, dm[...])
            sib_out[DOWN][pl.ds(8 * h, 8)] = r.reshape(8, 64, D).astype(BF16)
            sib_copy(DOWN, h).start()

        def ours(h):
            left = act[:, pl.ds(pl.multiple_of(h * 1024 + c * 512, 512), 512)]
            r = dot_tn(left, dm[...])
            acc[DOWN][pl.ds(8 * h, 8)] = r.reshape(8, 64, D)

        loop(2, theirs)
        loop(2, ours)

    def feed_back():
        def body(n):
            part = whole[DOWN][n // 4, (n // 2) % 2, pl.ds(2 * (n % 2), 2)].reshape(256, D)
            low = (dot_nt(dm[...], part) * slope[:, cols(n, 256)].astype(F32)).astype(BF16)
            slope[:, cols(n, 256)] = low
            gsup[UPB : UPB + 1, cols(n, 256)] = jnp.sum(fold(low.astype(F32)), axis=0, keepdims=True)

        loop(8, body)

    def back_to(left, w):
        for h in range(2):
            part = whole[w][h].reshape(256, COLS[w])
            wide[:, h * 256 : (h + 1) * 256] = dot_nt(left[...], part)

    def norm_back(grads, hat, root, gain, gain_at, bias_at):
        gs16[gain_at : gain_at + 1, :] += jnp.sum(fold(grads * hat), axis=0, keepdims=True)
        gs16[bias_at : bias_at + 1, :] += jnp.sum(fold(grads), axis=0, keepdims=True)
        scaled = grads * gain
        mean = jnp.mean(scaled, axis=-1, keepdims=True)
        along = jnp.mean(scaled * hat, axis=-1, keepdims=True)
        return (scaled - mean - hat * along) * root

    def second_back():
        gain = vec16[GAIN2 : GAIN2 + 1, :]

        def body(i):
            at = tile_rows(i)
            part = norm_back(wide[at, :], xh2[at, :], rs2[at, 0:1], gain, GAIN2, BIAS2)
            total = dm[at, :].astype(F32) + part
            x1[at, :] = total
            low = total.astype(BF16)
            dao[at, :] = low
            gs16[OUTB : OUTB + 1, :] += jnp.sum(fold(low.astype(F32)), axis=0, keepdims=True)

        loop(tiles, body)

    def first_back():
        gain = vec16[GAIN1 : GAIN1 + 1, :]

        def body(i):
            at = tile_rows(i)
            part = norm_back(wide[at, :], xh1[at, :], rs1[at, 0:1], gain, GAIN1, BIAS1)
            stage_part = x1[at, :] + part
            for h in range(4):
                stage[h, strided(i), :] = stage_part[:, h * 128 : (h + 1) * 128]

        loop(tiles, body)
        narrow(cotb)

    for w in (SM, QKV, OUT, UP, DOWN):
        own_shard(w)
    pl.semaphore_wait(barrier, 6)
    for w in (SM, QKV, OUT, UP, DOWN):
        g_start(w)
    constants()
    tok_copy.wait()
    first_norm()
    cot_copy.wait()
    cotangent_in()
    for w in (SM, QKV, OUT, UP, DOWN):
        g_z(w)
    for w in (SM, QKV):
        g_f(w)
    for w in (SM, QKV):
        g_s(w)
    g_f(OUT)
    g_f(UP)
    g_sib(SM)
    small_vectors()
    first_affine()
    g_sib(QKV)
    project_in()
    g_s(OUT)
    g_f(DOWN)
    loop(seqs // CHUNK, attention)
    g_s(UP)
    g_sib(OUT)
    project_out()
    second_norm()
    g_sib(UP)
    feed_up()
    g_s(DOWN)
    down_grad()
    g_sib(DOWN)
    feed_down()
    mixed_copy = pltpu.make_async_copy(tokb, mixed_hbm, io_sem.at[2])
    mixed_copy.start()
    r_1(DOWN)
    feed_back()
    r_2(DOWN)
    weight_grad(UP, a2, slope, 128, 512)
    r_3(DOWN)
    back_to(slope, UP)
    r_1(UP)
    second_back()
    r_4(DOWN)
    r_2(UP)
    weight_grad(OUT, ctx, dao, 128, 512)
    back_to(dao, OUT)
    r_1(OUT)
    r_3(UP)
    loop(seqs // CHUNK, attention_back)
    r_2(OUT)
    r_4(UP)
    weight_grad(QKV, a1, dpre, 128, 512)
    r_3(OUT)
    back_to(dpre, QKV)
    r_1(QKV)
    first_back()
    tgrad_copy = pltpu.make_async_copy(cotb, tgrad_hbm, io_sem.at[3])
    tgrad_copy.start()
    small_grads()
    r_4(OUT)
    r_2(QKV)
    r_1(SM)
    r_2(SM)
    r_3(QKV)
    r_3(SM)
    r_4(QKV)
    r_4(SM)
    for w in (SM, QKV, OUT, UP, DOWN):
        g_end(w)
        r_end(w)
    mixed_copy.wait()
    tgrad_copy.wait()


def call_layer(split, tokens, frames, small, shards, cotangent):
    count = tokens.shape[0]
    any_spec = pl.BlockSpec(memory_space=pl.ANY)
    vmem = pl.BlockSpec(memory_space=pltpu.VMEM)

    def kept(n, dtype=None):
        return [pltpu.VMEM((n, r, k), dtype or t) for r, k, t in zip(ROWS, COLS, KEPT)]

    scratch = [pltpu.VMEM((2, 2, 4, 2, r, k), t) for r, k, t in zip(ROWS, COLS, KEPT)]
    scratch += kept(16, F32)
    for n in (16, 8, 4, 3):
        scratch += kept(n) + kept(n)
    rows_bf = lambda k: pltpu.VMEM((count, k), BF16)
    rows_f = lambda k: pltpu.VMEM((count, k), F32)
    scratch += [
        rows_bf(D), rows_bf(D), pltpu.VMEM((4, count, 128), F32), rows_bf(D), rows_bf(D),
        rows_f(D), rows_f(D), rows_f(128), rows_f(128),
        rows_bf(D), rows_bf(D), rows_bf(3 * D),
        pltpu.VMEM((len(PAIRS), count // FRAMES, 128), F32),
        rows_bf(D), rows_f(D), rows_bf(FF), rows_bf(FF),
        rows_f(D), rows_bf(D), rows_bf(3 * D),
    ]
    scratch += [
        pltpu.VMEM((8, 512), F32), pltpu.VMEM((8, 1024), F32), pltpu.VMEM((8, 2048), F32), pltpu.VMEM((1, 3 * D), F32),
        pltpu.VMEM((count // FRAMES, 128), F32), pltpu.VMEM((D, 128), BF16), pltpu.VMEM((128, D), BF16),
        pltpu.VMEM((8, 512), F32), pltpu.VMEM((8, 1024), F32), pltpu.VMEM((8, 2048), F32),
        pltpu.VMEM((2, 2, 8, 8, 128), F32),
    ]
    scratch += [pltpu.SemaphoreType.DMA((5, 19))] * 2 + [pltpu.SemaphoreType.DMA((5, 17))] * 2
    scratch += [pltpu.SemaphoreType.DMA((4,))]
    out_shape = [jax.ShapeDtypeStruct(tokens.shape, BF16)] * 2
    out_shape += [jax.ShapeDtypeStruct((1, n), F32) for n in SMALL]
    out_shape += [jax.ShapeDtypeStruct(s.shape, F32) for s in shards]

    def body(*refs):
        layer_kernel(split, count, *refs)

    return pl.pallas_call(
        body,
        name="layer",
        out_shape=out_shape,
        in_specs=[any_spec, any_spec] + [vmem] * 13,
        out_specs=[any_spec, any_spec] + [vmem] * 12,
        scratch_shapes=scratch,
        compiler_params=pltpu.CompilerParams(
            collective_id=0, has_side_effects=True, vmem_limit_bytes=63 << 20
        ),
        cost_estimate=pl.CostEstimate(
            flops=2 * 3 * count * (3 * D * D + D * D + 2 * D * FF), bytes_accessed=1 << 23, transcendentals=count * FF
        ),
    )(tokens, cotangent, frames, *small, *shards)


def local(split, tokens, frames, g1, b1, wqkv, bqv, wo, bo, g2, b2, w1, b1f, w2, b2f, cotangent):
    spot = lax.axis_index("fsdp") // split

    def block(values):
        if split == 1:
            return values
        n = values.shape[0]
        every = lax.all_gather(values, "fsdp", axis=0, tiled=True)
        return lax.dynamic_slice(every, (spot * split * n,), (split * n,))

    def owned(values):
        if split == 1:
            return values
        n = values.shape[0]
        spread = lax.dynamic_update_slice(jnp.zeros((8 * n,), F32), values, (spot * n,))
        return lax.psum_scatter(spread, "fsdp", scatter_dimension=0, tiled=True)

    small = [block(v).reshape(1, -1) for v in (g1, b1, bqv, bo, g2, b2, b1f, b2f)]
    shards = [block(v).reshape(-1, 128) for v in (wqkv, wo, w1, w2)]
    outs = call_layer(split, tokens, frames.reshape(1, -1), small, shards, cotangent)
    mixed, tokens_grad = outs[:2]
    dg1, db1, dbqv, dbo, dg2, db2, db1f, db2f = [owned(v.reshape(-1)) for v in outs[2:10]]
    dwqkv, dwo, dw1, dw2 = [owned(v.reshape(-1)) for v in outs[10:]]
    return (mixed, tokens_grad, dg1, db1, dwqkv, dbqv, dwo, dbo, dg2, db2, dw1, db1f, dw2, db2f)


def solution(mesh):
    split = mesh.shape["fsdp"] // 8
    flat, rows = P(("dp", "fsdp")), P(("dp", "fsdp"), None)

    def body(*args):
        return local(split, *args)

    return jax.shard_map(
        body,
        mesh=mesh,
        in_specs=(rows,) + (flat,) * 13 + (rows,),
        out_specs=(rows, rows) + (flat,) * 12,
        check_vma=False,
    )
```

time: 600 us -> 130 us (0.22)
  waiting for transfers between devices: 171 us -> 0 us
  blocking collectives: 151 us -> 0 us
  matrix products: 122 us -> 0 us
  Pallas kernels: 0 us -> 118 us
  local copies, waits for them, and re-layouts: 102 us -> 10.4 us
  other arithmetic: 32.9 us -> 0 us
  between operations: 14.8 us -> 0.69 us
    unnamed x5 -> x0, waiting for transfers between devices: 168 us -> none
    dot_general x18 -> x0, matrix products: 122 us -> none  [the longest x3 44.2 us: attend(): return jnp.einsum('shtu,suhe->sthe', weights, values_in, precision=PRECISE)]
    pallas_call x0 -> x1, Pallas kernels: none -> 118 us  [call_layer(): pl.pallas_call(body, name='layer', out_shape=out_shape, in_specs=[any_spe...]
    unnamed x2 -> x0, blocking collectives: 78.4 us -> none
    all_gather x1 -> x0, blocking collectives: 72.9 us -> none  [local(): lax.all_gather(attn_low[4], ('dp', 'fsdp'), axis=0, tiled=True)]
    reshape x6 -> x0, local copies, waits for them, and re-layouts: 25.5 us -> none  [the longest x1 8.17 us: local(): packed.reshape(seqs_here, FRAMES, 3, HEADS, HEAD_DIM).astype(jnp.float32)]
    convert_element_type x4 -> x0, local copies, waits for them, and re-layouts: 20.6 us -> none  [the longest x2 18.1 us: local(): packed_grad = jnp.stack([query_grad, key_grad, value_grad], axis=2).resha...]
    reduce_sum x10 -> x0, other arithmetic: 17.9 us -> none  [the longest x1 8.47 us: attend(): weights = jnp.exp(scores - highest)]
  transfers between devices with their start and end apart: 4 -> 0, of which waited for: 2 -> 0; matrix products, arithmetic and copies ran while one was open for 14% -> 0% of each run, Pallas kernels for 0% -> 0%
where the time goes in v1:
time: 130 us
  Pallas kernels  118 us (91%)
  local copies, waits for them, and re-layouts  10.4 us (8%)
    pallas_call x1, Pallas kernels, call_layer(): pl.pallas_call(body, name='layer', out_shape=out_shape, in_specs=[any_spe...  118 us
    unnamed x40, local copies, waits for them, and re-layouts  10.4 us

profile of v1, /device:TPU:0, one launch (start us, length us, event | category | flops | bytes accessed | tf_op | source)
XLA Modules:
  0.0 129.5 jit_solution(6109840046382805015)
XLA Ops:
  0.7 118.4 %layer.1 = (bf16[960,512]{1,0:T(8,128)(2,1)}, bf16[960,512]{1,0:T(8,128)(2,1)}, f32[1,16]{1,0:T(1,128)}, f32[1,16]{1,0:T(1,128)}, f32[1,32]{1,0:T(1,128)}, /*ind...) custom-call(bf16[960,512]{1,0:T(8,128)(2,1)} %refs_0_.1, ...), custom_call_target="tpu_custom_call" | custom-call | flops 18119393280 | bytes 8388608 | tf_op jit(solution)/shard_map/layer/pallas_call | solution.py:715
  119.1 0.0 copy-start
  119.1 2.3 %copy.43 = bf16[960,512]{1,0:T(8,128)(2,1)} copy(bf16[960,512]{1,0:T(8,128)(2,1)} %get-tuple-element.56) | data formatting | bytes 1966080
  121.4 0.0 copy-done
  121.4 0.0 copy-start.12
  121.4 0.0 copy-start.3
  121.4 0.9 copy.44
  122.3 0.0 copy-done.12
  122.3 0.0 copy-start.11
  122.3 0.5 copy.45
  122.8 0.2 copy-done.11
  123.0 0.5 copy.46
  123.5 0.0 copy-done.3
  123.5 0.6 copy.47
  124.2 0.0 copy-done.10
  124.2 0.5 copy.48
  124.7 0.0 copy-done.4
  124.7 0.6 copy.49
  125.3 0.0 copy-done.9
  125.3 0.5 copy.50
  125.9 0.1 copy-done.8
  125.9 0.5 copy.51
  126.5 0.1 copy-done.7
  126.6 0.5 copy.52
  127.1 0.0 copy-done.2
  127.1 0.7 copy.53
  127.8 0.0 copy-done.6
  127.8 0.5 copy.54
  128.3 0.0 copy-done.1
  128.3 0.7 copy.55
  129.0 0.0 copy-done.5
  129.0 0.5 copy.56
  (9 shorter events, 0.0 us)
Async XLA Ops:
  119.1 2.3 %copy-start = (bf16[960,512]{1,0:T(8,128)(2,1)S(1)}, bf16[960,512]{1,0:T(8,128)(2,1)}, u32[]{:S(2)}) copy-start(bf16[960,512]{1,0:T(8,128)(2,1)} %get-tuple-element.57) | copy-start | bytes 2949124
  121.4 1.0 copy-start.12
  121.4 2.1 %copy-start.3 = (f32[192,128]{1,0:T(8,128)S(1)}, f32[192,128]{1,0:T(8,128)}, u32[]{:S(2)}) copy-start(f32[192,128]{1,0:T(8,128)} %get-tuple-element.32) | copy-start | bytes 294916
  122.3 0.7 copy-start.11
  123.5 0.7 copy-start.10
  123.5 1.2 copy-start.4
  123.5 3.6 %copy-start.2 = (f32[256,128]{1,0:T(8,128)S(1)}, f32[256,128]{1,0:T(8,128)}, u32[]{:S(2)}) copy-start(f32[256,128]{1,0:T(8,128)} %get-tuple-element.38) | copy-start | bytes 393220
  124.7 0.7 copy-start.9
  125.3 0.6 copy-start.8
  125.9 0.7 copy-start.7
  127.1 0.7 copy-start.6
  127.1 1.2 copy-start.1
  128.3 0.7 copy-start.5

commit v2 on v1

v2 whole, which is shorter than its diff:
```python
import math

import jax
import jax.numpy as jnp
from jax import lax
from jax.experimental import pallas as pl
from jax.experimental.pallas import tpu as pltpu
from jax.sharding import PartitionSpec as P

D = 512
HEADS = 8
HEAD_DIM = 64
FF = 2048
FRAMES = 5
EPSILON = 1e-05
PAIRS = [(t, u) for t in range(FRAMES) for u in range(t + 1)]

F32 = jnp.float32
BF16 = jnp.bfloat16
MESH = pl.DeviceIdType.MESH

SM, QA, QB, OUT, UP, DOWN = range(6)
ROWS = (8, 16, 16, 16, 16, 64)
COLS = (128, 3 * D // 2, 3 * D // 2, D, FF, D)
KEPT = (F32, BF16, BF16, BF16, BF16, BF16)
DIRECT = (SM, QA, QB)
HALF = D // 2
GROUP = HEADS // 2
QKV_ARG, OUT_ARG, UP_ARG, DOWN_ARG = range(4)
ARG = (None, QKV_ARG, QKV_ARG, OUT_ARG, UP_ARG, DOWN_ARG)
PACKED = (192, 64, 256, 256)
PACK = (0, 192, 256, 512)
PACK_SMALL, PACK_ALL = 768, 776
SMALL = (16, 16, 32, 16, 16, 16, 64, 16)
GAIN1, BIAS1, QVB, OUTB, GAIN2, BIAS2, UPB, DOWNB = range(8)

TILE = 192
CHUNK = 64


def dot(left, right):
    return lax.dot_general(left, right, (((1,), (0,)), ((), ())), preferred_element_type=F32)


def dot_nt(left, right):
    return lax.dot_general(left, right, (((1,), (1,)), ((), ())), preferred_element_type=F32)


def dot_tn(left, right):
    return lax.dot_general(left, right, (((0,), (0,)), ((), ())), preferred_element_type=F32)


def iota(shape, dim):
    return lax.broadcasted_iota(jnp.int32, shape, dim)


def fold(values):
    rows, cols = values.shape
    return jnp.sum(values.reshape(rows // 8, 8, cols), axis=0)


def split_two(values):
    high = values.astype(BF16)
    return high, (values - high.astype(F32)).astype(BF16)


def layer_kernel(split, count, *refs):
    refs = list(refs)

    def take(n):
        head = refs[:n]
        del refs[:n]
        return head

    tok_hbm, cot_hbm, frames_ref = take(3)
    small_in = take(8)
    shard_hbm = take(4)
    mixed_hbm, tgrad_hbm, grads_hbm = take(3)
    shard_in = take(4)
    (grads,) = take(1)
    whole = take(6)
    acc = take(6)
    sib_out, sib_in = take(6), take(6)
    two_out, two_in = take(6), take(6)
    one_out, one_in = take(6), take(6)
    zed_out, zed_in = take(6), take(6)
    (tokb, cotb, stage, xt, dm, xh1, xh2, rs1, rs2, a1, a2, qkv, prob, ctx, x1, act, slope, wide, dao, dpre, turned) = take(21)
    (vec16, vecqv, vecup, biasq, living, pick, pick_t, gs16, gsqv, gsup, sums) = take(11)
    (gsend, grecv, rsend, rrecv, io_sem) = take(5)

    seqs = count // FRAMES
    dp = lax.axis_index("dp")
    fs = lax.axis_index("fsdp")
    x, c = dp // 2, dp % 2
    group, rest = fs // split, fs % split
    z, y = group // 2, group % 2

    def device(x_, c_, z_, y_):
        return (x_ * 2 + c_, (z_ * 2 + y_) * split + rest)

    first = x + c * (y - x)
    second = y + c * (x - y)

    def to_xy(f_, s_):
        return f_ + c * (s_ - f_), s_ + c * (f_ - s_)

    def peer(f_, s_):
        x_, y_ = to_xy(f_, s_)
        return device(x_, c, z, y_)

    sibling = device(x, 1 - c, z, y)
    first_dev = peer(1 - first, second)
    second_dev = peer(first, 1 - second)
    across_dev = peer(1 - first, 1 - second)
    zeds = (z + 1 - 2 * (z % 2), (z + 2) % 4, 3 - z)
    zed_dev = [device(x, c, zk, y) for zk in zeds]

    tok_copy = pltpu.make_async_copy(tok_hbm, tokb, io_sem.at[0])
    cot_copy = pltpu.make_async_copy(cot_hbm, cotb, io_sem.at[1])
    shard_copy = [pltpu.make_async_copy(shard_hbm[k], shard_in[k], io_sem.at[4 + k]) for k in range(4)]
    for copy in shard_copy:
        copy.start()
    tok_copy.start()
    cot_copy.start()
    barrier = pltpu.get_barrier_semaphore()
    for dev in [sibling, first_dev, second_dev, across_dev] + zed_dev:
        pl.semaphore_signal(barrier, inc=1, device_id=dev, device_id_type=MESH)

    def shard(w, f_, s_, z_):
        x_, y_ = to_xy(f_, s_)
        return whole[w].at[x_, c, z_, y_]

    def line(w, f_, s_):
        x_, y_ = to_xy(f_, s_)
        return whole[w].at[x_, c, :, y_]

    def gcopy(w, sent, got, ref, dev):
        return pltpu.make_async_remote_copy(
            src_ref=ref, dst_ref=ref, send_sem=gsend.at[w, sent], recv_sem=grecv.at[w, got], device_id=dev, device_id_type=MESH
        )

    def cols_of(w):
        if w in (QA, QB):
            return [(4 * p + 2 * (w - QA) + b, 2 * p + b) for p in range(3) for b in range(2)]
        return [(k, k) for k in range(COLS[w] // 128)]

    def own_shard(w):
        if w == SM:
            whole[w][x, c, z, y] = jnp.zeros((8, 128), F32)
            for p, n in enumerate(SMALL):
                whole[w][x, c, z, y, p : p + 1, 0:n] = small_in[p][...].astype(BF16).astype(F32)
        else:
            if w != QB:
                shard_copy[ARG[w]].wait()
            step = PACKED[ARG[w]] // ROWS[w]
            for k, to in cols_of(w):
                part = shard_in[ARG[w]][pl.ds(k, ROWS[w], stride=step), :]
                whole[w][x, c, z, y, :, to * 128 : (to + 1) * 128] = part.astype(BF16)

    def hand_on(w, ref, spot):
        if w in DIRECT:
            gcopy(w, 1, 3, ref, first_dev).start()
            gcopy(w, 2, 7, ref, second_dev).start()
            gcopy(w, 3, 8, ref, across_dev).start()
        else:
            gcopy(w, 1, 3 + spot, ref, first_dev).start()
            gcopy(w, 2, 7, ref, second_dev).start()

    def to_sibling(w, f_, s_):
        gcopy(w, 4, 9, line(w, f_, s_), sibling).start()

    def g_start(w):
        ref = shard(w, first, second, z)
        for k in range(3):
            gcopy(w, 0, k, ref, zed_dev[k]).start()
        hand_on(w, ref, z)

    def g_z(w):
        for k in range(3):
            ref = shard(w, first, second, zeds[k])
            gcopy(w, 0, k, ref, zed_dev[k]).wait_recv()
            hand_on(w, ref, zeds[k])
        to_sibling(w, first, second)

    def g_f(w):
        for k in range(4):
            ref = shard(w, 1 - first, second, k)
            gcopy(w, 1, 3 + k, ref, first_dev).wait_recv()
            gcopy(w, 2, 8, ref, second_dev).start()
        to_sibling(w, 1 - first, second)

    def g_s(w):
        if w in DIRECT:
            gcopy(w, 1, 3, line(w, 1 - first, second), first_dev).wait_recv()
            to_sibling(w, 1 - first, second)
        gcopy(w, 2, 7, line(w, first, 1 - second), second_dev).wait_recv()
        to_sibling(w, first, 1 - second)
        gcopy(w, 2, 8, line(w, 1 - first, 1 - second), second_dev).wait_recv()
        to_sibling(w, 1 - first, 1 - second)

    def g_sib(w):
        ref = whole[w].at[:, 1 - c]
        gcopy(w, 4, 9, ref, sibling).wait_recv()

    def g_end(w):
        gcopy(w, 0, 0, zed_out[w], sibling).wait_send()
        four = line(w, first, second)
        gcopy(w, 1, 3, four, sibling).wait_send()
        if w in DIRECT:
            gcopy(w, 2, 7, four, sibling).wait_send()
            gcopy(w, 3, 8, four, sibling).wait_send()
        else:
            gcopy(w, 2, 7, two_out[w], sibling).wait_send()
        gcopy(w, 4, 9, sib_out[w], sibling).wait_send()

    def loop(n, body, start=0):
        def step(i, carry):
            body(i)
            return carry

        lax.fori_loop(start, n, step, 0)

    def place(f_, s_, z_):
        x_, y_ = to_xy(f_, s_)
        return x_ * 8 + z_ * 2 + y_

    def rcopy(w, sent, got, src, dst, dev):
        return pltpu.make_async_remote_copy(
            src_ref=src, dst_ref=dst, send_sem=rsend.at[w, sent], recv_sem=rrecv.at[w, got], device_id=dev, device_id_type=MESH
        )

    def sib_copy(w, at, n):
        return rcopy(w, 0, 0, sib_out[w].at[pl.ds(at, n)], sib_in[w].at[pl.ds(at, n)], sibling)

    def two_copy(w, k, got):
        return rcopy(w, 1, got, two_out[w].at[k], two_in[w].at[k], second_dev)

    def one_copy(w, k):
        return rcopy(w, 2, 6 + k, one_out[w].at[k], one_in[w].at[k], first_dev)

    def zed_copy(w, k):
        return rcopy(w, 3, 10, zed_out[w].at[k], zed_in[w].at[k], zed_dev[k])

    def r_1(w):
        sib_copy(w, 0, 16).wait_recv()

        def step(k, got):
            j = place(k // 4, 1 - second, k % 4)
            two_out[w][k] = (acc[w][j] + sib_in[w][j].astype(F32)).astype(KEPT[w])
            two_copy(w, k, got).start()

        loop(4, lambda i: step(4 * (1 - first) + i, 1 + i))
        loop(4, lambda i: step(4 * first + i, 5))

    def r_2(w):
        def step(i):
            k = (z + 1 + i) % 4
            j = place(1 - first, second, k)
            slot = (1 - first) * 4 + k
            two_copy(w, slot, 1 + k).wait_recv()
            total = acc[w][j] + sib_in[w][j].astype(F32) + two_in[w][slot].astype(F32)
            one_out[w][k] = total.astype(KEPT[w])
            one_copy(w, k).start()

        loop(4, step)

    def r_3(w):
        line_in = two_in[w].at[pl.ds(4 * first, 4)]
        rcopy(w, 1, 5, line_in, line_in, second_dev).wait_recv()
        for k in range(3):
            j = place(first, second, zeds[k])
            slot = first * 4 + zeds[k]
            one_copy(w, zeds[k]).wait_recv()
            total = acc[w][j] + sib_in[w][j].astype(F32) + two_in[w][slot].astype(F32) + one_in[w][zeds[k]].astype(F32)
            zed_out[w][k] = total.astype(KEPT[w])
            zed_copy(w, k).start()

    def grad_copy(at, rows, k):
        return pltpu.make_async_copy(grads.at[pl.ds(at, rows)], grads_hbm.at[pl.ds(at, rows)], io_sem.at[8 + k])

    def arg_copy(k):
        return grad_copy(PACK[k], PACKED[k], k)

    small_copy = grad_copy(PACK_SMALL, 8, 4)

    def r_4(w):
        j = place(first, second, z)
        slot = first * 4 + z
        one_copy(w, z).wait_recv()
        total = acc[w][j] + sib_in[w][j].astype(F32) + two_in[w][slot].astype(F32) + one_in[w][z].astype(F32)
        rcopy(w, 3, 10, zed_in[w], zed_in[w], sibling).wait_recv()
        for k in range(3):
            total = total + zed_in[w][k].astype(F32)
        if w == SM:
            grads[PACK_SMALL:PACK_ALL, :] = total
            small_copy.start()
        else:
            step = PACKED[ARG[w]] // ROWS[w]
            for k, at in cols_of(w):
                grads[pl.ds(PACK[ARG[w]] + k, ROWS[w], stride=step), :] = total[:, at * 128 : (at + 1) * 128]

    def r_end(w):
        sib_copy(w, 0, 16).wait_send()
        rcopy(w, 1, 5, two_out[w], two_in[w], sibling).wait_send()
        rcopy(w, 2, 6, one_out[w], one_in[w], sibling).wait_send()
        rcopy(w, 3, 10, zed_out[w], zed_in[w], sibling).wait_send()

    tiles = count // TILE
    per_frame = seqs // TILE

    def tile_rows(i):
        return pl.ds(pl.multiple_of(i * TILE, TILE), TILE)

    def strided(i):
        return pl.ds(i // per_frame + FRAMES * TILE * (i % per_frame), TILE, stride=FRAMES)

    def widen(src):
        def body(i):
            for h in range(4):
                stage[h, tile_rows(i), :] = src[tile_rows(i), h * 128 : (h + 1) * 128].astype(F32)

        loop(tiles, body)

    def narrow(dst):
        def body(i):
            for h in range(4):
                dst[tile_rows(i), h * 128 : (h + 1) * 128] = stage[h, tile_rows(i), :].astype(BF16)

        loop(tiles, body)

    def center(values):
        mean = jnp.mean(values, axis=-1, keepdims=True)
        centered = values - mean
        root = lax.rsqrt(jnp.mean(centered * centered, axis=-1, keepdims=True) + EPSILON)
        return centered * root, root

    def constants():
        lane, row = iota((HALF, 128), 1), iota((HALF, 128), 0)
        pick[...] = jnp.where((row // HEAD_DIM == lane % GROUP) & (lane < 2 * GROUP), 1.0, 0.0).astype(BF16)
        lane, row = iota((128, HALF), 1), iota((128, HALF), 0)
        pick_t[...] = jnp.where((lane // HEAD_DIM == row % GROUP) & (row < 2 * GROUP), 1.0, 0.0).astype(BF16)
        same = iota((seqs, seqs), 0) == iota((seqs, seqs), 1)
        wide_frames = jnp.broadcast_to(frames_ref[...].astype(F32), (seqs, seqs))
        spread = jnp.where(same, wide_frames, 0.0).astype(BF16)
        living[...] = dot(spread, jnp.ones((seqs, 128), BF16))
        gs16[...] = jnp.zeros_like(gs16)
        gsqv[...] = jnp.zeros_like(gsqv)
        gsup[...] = jnp.zeros_like(gsup)

    def first_norm():
        widen(tokb)

        def body(i):
            values = jnp.concatenate([stage[h, strided(i), :] for h in range(4)], axis=1)
            xt[tile_rows(i), :] = values.astype(BF16)
            hat, root = center(values)
            xh1[tile_rows(i), :] = hat
            rs1[tile_rows(i), :] = jnp.broadcast_to(root, (TILE, 128))

        loop(tiles, body)

    def cotangent_in():
        widen(cotb)

        def body(i):
            values = jnp.concatenate([stage[h, strided(i), :] for h in range(4)], axis=1)
            dm[tile_rows(i), :] = values.astype(BF16)
            gs16[DOWNB : DOWNB + 1, :] += jnp.sum(fold(values), axis=0, keepdims=True)

        loop(tiles, body)

    def small_vectors():
        raw = whole[SM][...].reshape(256, 128).astype(BF16)
        for n, dst in ((16, vec16), (32, vecqv), (64, vecup)):
            width = 32 * n
            for at in range(0, width, 512):
                near = iota((128, 512), 0) == (iota((128, 512), 1) + at) % n
                spread = dot(raw, jnp.where(near, 1.0, 0.0).astype(BF16))
                mine = iota((256, 512), 0) // 8 == (iota((256, 512), 1) + at) // n
                dst[:, at : at + 512] = jnp.sum(jnp.where(mine, spread, 0.0).reshape(32, 8, 512), axis=0)
        biasq[...] = jnp.zeros_like(biasq)
        for h in range(2):
            for part in range(2):
                at = 3 * HALF * h + 2 * HALF * part
                biasq[:, at : at + HALF] = vecqv[QVB : QVB + 1, part * D + h * HALF : part * D + (h + 1) * HALF]

    def small_grads():
        for n, src in ((16, gs16), (32, gsqv), (64, gsup)):
            width = 32 * n
            for at in range(0, width, 512):
                mine = iota((256, 512), 0) // 8 == (iota((256, 512), 1) + at) // n
                values = jnp.broadcast_to(src[:, at : at + 512][None], (32, 8, 512)).reshape(256, 512)
                high, low = split_two(jnp.where(mine, values, 0.0))
                near = jnp.where(iota((128, 512), 0) == (iota((128, 512), 1) + at) % n, 1.0, 0.0).astype(BF16)
                part = dot_nt(high, near) + dot_nt(low, near)
                total = part if n == 16 and at == 0 else total + part
        sums[...] = total.reshape(2, 2, 8, 8, 128)
        for h in range(2):
            acc[SM][8 * h : 8 * h + 8] = sums[h, c]
            sib_out[SM][8 * h : 8 * h + 8] = sums[h, 1 - c]
            sib_copy(SM, 8 * h, 8).start()

    def first_affine():
        gain, bias = vec16[GAIN1 : GAIN1 + 1, :], vec16[BIAS1 : BIAS1 + 1, :]

        def body(i):
            a1[tile_rows(i), :] = (xh1[tile_rows(i), :] * gain + bias).astype(BF16)

        loop(tiles, body)

    def cols(n, width):
        return pl.ds(pl.multiple_of(n * width, width), width)

    def matrix_cols(w, n, width):
        part = whole[w][:, :, :, :, :, cols(n, width)]
        return part.reshape(32 * ROWS[w], width)

    def matrix(w):
        return whole[w][...].reshape(32 * ROWS[w], COLS[w])

    def project_in(h):
        def body(n):
            at = cols(n + 3 * h, HALF)
            r = dot(a1[...], matrix_cols(QA + h, n, HALF)) + biasq[:, at]
            qkv[:, at] = r.astype(BF16)

        loop(3, body)

    def frame_rows(t, i):
        return pl.ds(pl.multiple_of(t * seqs + i * CHUNK, CHUNK), CHUNK)

    def heads_of(h, i, part):
        at = (3 * h + part) * HALF
        return [qkv[frame_rows(t, i), at : at + HALF].astype(F32) for t in range(FRAMES)]

    def spread_heads(parts):
        lanes = iota((CHUNK, 128), 1)
        mixed_parts = []
        for part in parts:
            high, low = split_two(part)
            mixed_parts.append(jnp.where(lanes < GROUP, high.astype(F32), low.astype(F32)).astype(BF16))
        return dot(jnp.concatenate(mixed_parts, axis=0), pick_t[...])

    def rows_of(values, k):
        return values[k * CHUNK : (k + 1) * CHUNK]

    def attention(h, i):
        q, k_, v = heads_of(h, i, 0), heads_of(h, i, 1), heads_of(h, i, 2)
        halves = [split_two(q[t] * k_[u]) for t, u in PAIRS]
        high = jnp.concatenate([h for h, _ in halves], axis=0)
        low = jnp.concatenate([l for _, l in halves], axis=0)
        scores = (dot(high, pick[...]) + dot(low, pick[...])) * (1.0 / math.sqrt(HEAD_DIM))
        live = living[pl.ds(pl.multiple_of(i * CHUNK, CHUNK), CHUNK), :]
        weights = []
        for t in range(FRAMES):
            row = [rows_of(scores, PAIRS.index((t, u))) for u in range(t + 1)]
            row = [jnp.where(u < live, part, -1e30) for u, part in enumerate(row)]
            top = row[0]
            for part in row[1:]:
                top = jnp.maximum(top, part)
            row = [jnp.exp(part - top) for part in row]
            total = row[0]
            for part in row[1:]:
                total = total + part
            weights += [part / total for part in row]
        for k, part in enumerate(weights):
            prob[h, k, pl.ds(pl.multiple_of(i * CHUNK, CHUNK), CHUNK), :] = part
        spread = spread_heads(weights)
        for t in range(FRAMES):
            total = rows_of(spread, PAIRS.index((t, 0))) * v[0]
            for u in range(1, t + 1):
                total = total + rows_of(spread, PAIRS.index((t, u))) * v[u]
            ctx[frame_rows(t, i), h * HALF : (h + 1) * HALF] = total.astype(BF16)

    def attention_back(h, i):
        v = heads_of(h, i, 2)
        g = [wide[frame_rows(t, i), h * HALF : (h + 1) * HALF] for t in range(FRAMES)]
        base = 3 * HALF * h
        products = jnp.concatenate([(g[t] * v[u]).astype(BF16) for t, u in PAIRS], axis=0)
        slopes = dot(products, pick[...])
        weights = [prob[h, k, pl.ds(pl.multiple_of(i * CHUNK, CHUNK), CHUNK), :] for k in range(len(PAIRS))]
        scaled = []
        for t in range(FRAMES):
            ks = [PAIRS.index((t, u)) for u in range(t + 1)]
            mean = weights[ks[0]] * rows_of(slopes, ks[0])
            for k in ks[1:]:
                mean = mean + weights[k] * rows_of(slopes, k)
            scaled += [weights[k] * (rows_of(slopes, k) - mean) * (1.0 / math.sqrt(HEAD_DIM)) for k in ks]
        spread_p = spread_heads(weights)
        for u in range(FRAMES):
            total = None
            for t in range(u, FRAMES):
                part = rows_of(spread_p, PAIRS.index((t, u))) * g[t]
                total = part if total is None else total + part
            low = total.astype(BF16)
            dpre[frame_rows(u, i), base + 2 * HALF : base + 3 * HALF] = low
            gsqv[QVB : QVB + 1, D + h * HALF : D + (h + 1) * HALF] += jnp.sum(fold(low.astype(F32)), axis=0, keepdims=True)
        q, k_ = heads_of(h, i, 0), heads_of(h, i, 1)
        spread_s = spread_heads(scaled)
        for t in range(FRAMES):
            total = None
            for u in range(t + 1):
                part = rows_of(spread_s, PAIRS.index((t, u))) * k_[u]
                total = part if total is None else total + part
            low = total.astype(BF16)
            dpre[frame_rows(t, i), base : base + HALF] = low
            gsqv[QVB : QVB + 1, h * HALF : (h + 1) * HALF] += jnp.sum(fold(low.astype(F32)), axis=0, keepdims=True)
        for u in range(FRAMES):
            total = None
            for t in range(u, FRAMES):
                part = rows_of(spread_s, PAIRS.index((t, u))) * q[t]
                total = part if total is None else total + part
            dpre[frame_rows(u, i), base + HALF : base + 2 * HALF] = total.astype(BF16)

    def project_out():
        bias = vec16[OUTB : OUTB + 1, :]
        for n in range(2):
            at = slice(n * 256, (n + 1) * 256)
            r = dot(ctx[...], whole[OUT][:, :, :, :, :, at].reshape(D, 256))
            x1[:, at] = xt[:, at].astype(F32) + r + bias[:, at]

    def second_norm(start, stop):
        gain, bias = vec16[GAIN2 : GAIN2 + 1, :], vec16[BIAS2 : BIAS2 + 1, :]

        def body(i):
            hat, root = center(x1[tile_rows(i), :])
            xh2[tile_rows(i), :] = hat
            rs2[tile_rows(i), :] = jnp.broadcast_to(root, (TILE, 128))
            a2[tile_rows(i), :] = (hat * gain + bias).astype(BF16)

        loop(stop, body, start)

    def feed_up(start, stop):
        k0 = math.sqrt(2.0 / math.pi)
        k1 = k0 * 0.044715

        def body(n):
            f = dot(a2[...], matrix_cols(UP, n, 256)) + vecup[UPB : UPB + 1, cols(n, 256)]
            square = f * f
            half = 0.5 + 0.5 * jnp.tanh(f * (k0 + k1 * square))
            act[:, cols(n, 256)] = (f * half).astype(BF16)
            grow = half + (f * (half - half * half)) * (2.0 * k0 + 6.0 * k1 * square)
            slope[:, cols(n, 256)] = grow.astype(BF16)

        loop(stop, body, start)

    def feed_down(n):
        bias = vec16[DOWNB : DOWNB + 1, :]
        at = slice(n * 256, (n + 1) * 256)
        r = dot(act[...], whole[DOWN][:, :, :, :, :, at].reshape(FF, 256))
        r = r + x1[:, at] + bias[:, at]
        for t in range(FRAMES):
            for h in range(2):
                stage[2 * n + h, pl.ds(t, seqs, stride=FRAMES), :] = r[t * seqs : (t + 1) * seqs, h * 128 : (h + 1) * 128]

    def turn(left, core):
        parts = [left[:, pl.ds(pl.multiple_of(h * 256 + core * 128, 128), 128)] for h in range(2)]
        turned[...] = jnp.transpose(jnp.concatenate(parts, axis=1))

    def grad_theirs(w, left, right, base, width):
        turn(left, 1 - c)

        def body(n):
            r = dot(turned[...], right[:, cols(n + base, width)])
            sib_out[w][:, :, cols(n, width)] = r.reshape(16, ROWS[w], width).astype(BF16)

        loop(COLS[w] // width, body)
        sib_copy(w, 0, 16).start()

    def grad_ours(w, left, right, base, width):
        turn(left, c)

        def body(n):
            r = dot(turned[...], right[:, cols(n + base, width)])
            acc[w][:, :, cols(n, width)] = r.reshape(16, ROWS[w], width)

        loop(COLS[w] // width, body)

    def down_theirs(h):
        left = act[:, pl.ds(pl.multiple_of(h * 1024 + (1 - c) * 512, 512), 512)]
        r = dot_tn(left, dm[...])
        sib_out[DOWN][8 * h : 8 * h + 8] = r.reshape(8, 64, D).astype(BF16)
        sib_copy(DOWN, 8 * h, 8).start()

    def down_ours(h):
        left = act[:, pl.ds(pl.multiple_of(h * 1024 + c * 512, 512), 512)]
        acc[DOWN][8 * h : 8 * h + 8] = dot_tn(left, dm[...]).reshape(8, 64, D)

    def feed_back(start, stop):
        def body(n):
            part = whole[DOWN][n // 4, (n // 2) % 2, pl.ds(2 * (n % 2), 2)].reshape(256, D)
            low = (dot_nt(dm[...], part) * slope[:, cols(n, 256)].astype(F32)).astype(BF16)
            slope[:, cols(n, 256)] = low
            gsup[UPB : UPB + 1, cols(n, 256)] = jnp.sum(fold(low.astype(F32)), axis=0, keepdims=True)

        loop(stop, body, start)

    def back_to(left, w, h):
        wide[:, h * 256 : (h + 1) * 256] = dot_nt(left[...], whole[w][h].reshape(256, COLS[w]))

    def back_in(h):
        r = dot_nt(dpre[:, : 3 * HALF], whole[QA][h].reshape(256, 3 * HALF))
        r = r + dot_nt(dpre[:, 3 * HALF :], whole[QB][h].reshape(256, 3 * HALF))
        wide[:, h * 256 : (h + 1) * 256] = r

    def norm_back(grads, hat, root, gain, gain_at, bias_at):
        gs16[gain_at : gain_at + 1, :] += jnp.sum(fold(grads * hat), axis=0, keepdims=True)
        gs16[bias_at : bias_at + 1, :] += jnp.sum(fold(grads), axis=0, keepdims=True)
        scaled = grads * gain
        mean = jnp.mean(scaled, axis=-1, keepdims=True)
        along = jnp.mean(scaled * hat, axis=-1, keepdims=True)
        return (scaled - mean - hat * along) * root

    def second_back(start, stop):
        gain = vec16[GAIN2 : GAIN2 + 1, :]

        def body(i):
            at = tile_rows(i)
            part = norm_back(wide[at, :], xh2[at, :], rs2[at, 0:1], gain, GAIN2, BIAS2)
            total = dm[at, :].astype(F32) + part
            xh2[at, :] = total
            low = total.astype(BF16)
            dao[at, :] = low
            gs16[OUTB : OUTB + 1, :] += jnp.sum(fold(low.astype(F32)), axis=0, keepdims=True)

        loop(stop, body, start)

    def first_back():
        gain = vec16[GAIN1 : GAIN1 + 1, :]

        def body(i):
            at = tile_rows(i)
            part = norm_back(wide[at, :], xh1[at, :], rs1[at, 0:1], gain, GAIN1, BIAS1)
            stage_part = xh2[at, :] + part
            for h in range(4):
                stage[h, strided(i), :] = stage_part[:, h * 128 : (h + 1) * 128]

        loop(tiles, body)
        narrow(cotb)

    own_shard(SM)
    own_shard(QA)
    own_shard(QB)
    pl.semaphore_wait(barrier, 7)
    g_start(SM)
    g_start(QA)
    constants()
    tok_copy.wait()
    first_norm()
    own_shard(OUT)
    g_start(OUT)
    g_start(QB)
    own_shard(UP)
    g_start(UP)
    g_z(SM)
    g_z(QA)
    g_z(OUT)
    own_shard(DOWN)
    g_start(DOWN)
    g_s(SM)
    g_sib(SM)
    g_z(QB)
    g_s(QA)
    g_sib(QA)
    cot_copy.wait()
    cotangent_in()
    g_f(OUT)
    g_z(UP)
    g_s(QB)
    small_vectors()
    first_affine()
    project_in(0)
    loop(1, lambda i: attention(0, i), 0)
    g_sib(QB)
    g_f(UP)
    g_s(OUT)
    project_in(1)
    g_z(DOWN)
    loop(3, lambda i: attention(0, i), 1)
    loop(2, lambda i: attention(1, i), 0)
    g_sib(OUT)
    loop(3, lambda i: attention(1, i), 2)
    g_s(UP)
    project_out()
    second_norm(0, 5)
    g_f(DOWN)
    g_sib(UP)
    feed_up(0, 8)
    down_theirs(0)
    g_s(DOWN)
    down_theirs(1)
    down_ours(0)
    down_ours(1)
    g_sib(DOWN)
    feed_back(0, 4)
    r_1(DOWN)
    feed_back(4, 8)
    back_to(slope, UP, 0)
    grad_theirs(UP, a2, slope, 0, 512)
    grad_ours(UP, a2, slope, 0, 512)
    r_2(DOWN)
    back_to(slope, UP, 1)
    r_1(UP)
    second_back(0, 5)
    back_to(dao, OUT, 0)
    back_to(dao, OUT, 1)
    grad_ours(OUT, ctx, dao, 0, 512)
    loop(1, lambda i: attention_back(1, i), 0)
    grad_theirs(OUT, ctx, dao, 0, 512)
    loop(2, lambda i: attention_back(0, i), 0)
    r_3(DOWN)
    r_2(UP)
    loop(3, lambda i: attention_back(0, i), 2)
    r_1(OUT)
    grad_theirs(QA, a1, dpre, 0, HALF)
    loop(3, lambda i: attention_back(1, i), 1)
    grad_ours(QA, a1, dpre, 0, HALF)
    r_1(QA)
    grad_theirs(QB, a1, dpre, 3, HALF)
    r_3(UP)
    r_2(OUT)
    grad_ours(QB, a1, dpre, 3, HALF)
    back_in(0)
    r_1(QB)
    r_2(QA)
    back_in(1)
    first_back()
    tgrad_copy = pltpu.make_async_copy(cotb, tgrad_hbm, io_sem.at[3])
    tgrad_copy.start()
    small_grads()
    r_2(QB)
    r_3(QA)
    r_3(OUT)
    r_1(SM)
    r_3(QB)
    r_4(DOWN)
    arg_copy(DOWN_ARG).start()
    r_2(SM)
    r_3(SM)
    r_4(UP)
    arg_copy(UP_ARG).start()
    for w in (SM, QA, QB, OUT, UP, DOWN):
        g_end(w)
    r_4(QA)
    feed_down(0)
    feed_down(1)
    narrow(tokb)
    mixed_copy = pltpu.make_async_copy(tokb, mixed_hbm, io_sem.at[2])
    mixed_copy.start()
    r_4(OUT)
    arg_copy(OUT_ARG).start()
    r_4(SM)
    r_4(QB)
    arg_copy(QKV_ARG).start()
    for w in (SM, QA, QB, OUT, UP, DOWN):
        r_end(w)
    for k in range(4):
        arg_copy(k).wait()
    small_copy.wait()
    mixed_copy.wait()
    tgrad_copy.wait()


def call_layer(split, tokens, frames, small, shards, cotangent):
    count = tokens.shape[0]
    any_spec = pl.BlockSpec(memory_space=pl.ANY)
    vmem = pl.BlockSpec(memory_space=pltpu.VMEM)

    def kept(n, dtype=None):
        return [pltpu.VMEM((n, r, k), dtype or t) for r, k, t in zip(ROWS, COLS, KEPT)]

    scratch = [pltpu.VMEM((n, 128), F32) for n in PACKED] + [pltpu.VMEM((PACK_ALL, 128), F32)]
    scratch += [pltpu.VMEM((2, 2, 4, 2, r, k), t) for r, k, t in zip(ROWS, COLS, KEPT)]
    scratch += kept(16, F32)
    for n in (16, 8, 4, 3):
        scratch += kept(n) + kept(n)
    rows_bf = lambda k: pltpu.VMEM((count, k), BF16)
    rows_f = lambda k: pltpu.VMEM((count, k), F32)
    scratch += [
        rows_bf(D), rows_bf(D), pltpu.VMEM((4, count, 128), F32), rows_bf(D), rows_bf(D),
        rows_f(D), rows_f(D), rows_f(128), rows_f(128),
        rows_bf(D), rows_bf(D), rows_bf(3 * D),
        pltpu.VMEM((2, len(PAIRS), count // FRAMES, 128), F32),
        rows_bf(D), rows_f(D), rows_bf(FF), rows_bf(FF),
        rows_f(D), rows_bf(D), rows_bf(3 * D), pltpu.VMEM((HALF, count), BF16),
    ]
    scratch += [
        pltpu.VMEM((8, 512), F32), pltpu.VMEM((8, 1024), F32), pltpu.VMEM((8, 2048), F32), pltpu.VMEM((1, 3 * D), F32),
        pltpu.VMEM((count // FRAMES, 128), F32), pltpu.VMEM((HALF, 128), BF16), pltpu.VMEM((128, HALF), BF16),
        pltpu.VMEM((8, 512), F32), pltpu.VMEM((8, 1024), F32), pltpu.VMEM((8, 2048), F32),
        pltpu.VMEM((2, 2, 8, 8, 128), F32),
    ]
    scratch += [pltpu.SemaphoreType.DMA((6, n)) for n in (5, 10, 4, 11)]
    scratch += [pltpu.SemaphoreType.DMA((13,))]
    out_shape = [jax.ShapeDtypeStruct(tokens.shape, BF16)] * 2
    out_shape += [jax.ShapeDtypeStruct((PACK_ALL, 128), F32)]

    def body(*refs):
        layer_kernel(split, count, *refs)

    return pl.pallas_call(
        body,
        name="layer",
        out_shape=out_shape,
        in_specs=[any_spec, any_spec] + [vmem] * 9 + [any_spec] * 4,
        out_specs=[any_spec] * 3,
        scratch_shapes=scratch,
        compiler_params=pltpu.CompilerParams(
            collective_id=0, has_side_effects=True, vmem_limit_bytes=63 << 20
        ),
        cost_estimate=pl.CostEstimate(
            flops=2 * 3 * count * (3 * D * D + D * D + 2 * D * FF), bytes_accessed=1 << 23, transcendentals=count * FF
        ),
    )(tokens, cotangent, frames, *small, *shards)


def hand_out(mixed, tokens_grad, grads):
    any_spec = pl.BlockSpec(memory_space=pl.ANY)
    vmem = pl.BlockSpec(memory_space=pltpu.VMEM)

    def body(mixed_in, tgrad_in, grads_in, *refs):
        outs, (mixed_v, tgrad_v, grads_v, in_sem, out_sem) = refs[:14], refs[14:]
        smalls, big = outs[2:10], (outs[0], outs[1]) + tuple(outs[10:])
        reads = [
            pltpu.make_async_copy(src, dst, in_sem.at[k])
            for k, (src, dst) in enumerate(((mixed_in, mixed_v), (tgrad_in, tgrad_v), (grads_in, grads_v)))
        ]
        parts = [mixed_v, tgrad_v] + [grads_v.at[pl.ds(PACK[k], PACKED[k])] for k in range(4)]
        writes = [pltpu.make_async_copy(src, dst, out_sem.at[k]) for k, (src, dst) in enumerate(zip(parts, big))]
        for copy in reads:
            copy.start()
        for k in range(3):
            reads[k].wait()
            for copy in writes[2:] if k == 2 else writes[k : k + 1]:
                copy.start()
        for p, n in enumerate(SMALL):
            smalls[p][...] = grads_v[PACK_SMALL + p : PACK_SMALL + p + 1, 0:n]
        for copy in writes:
            copy.wait()

    row_shapes = [jax.ShapeDtypeStruct(mixed.shape, BF16)] * 2
    small_shapes = [jax.ShapeDtypeStruct((1, n), F32) for n in SMALL]
    shard_shapes = [jax.ShapeDtypeStruct((n, 128), F32) for n in PACKED]
    return pl.pallas_call(
        body,
        name="hand_out",
        out_shape=row_shapes + small_shapes + shard_shapes,
        in_specs=[any_spec] * 3,
        out_specs=[any_spec] * 2 + [vmem] * 8 + [any_spec] * 4,
        scratch_shapes=[
            pltpu.VMEM(mixed.shape, BF16), pltpu.VMEM(mixed.shape, BF16), pltpu.VMEM(grads.shape, F32),
            pltpu.SemaphoreType.DMA((3,)), pltpu.SemaphoreType.DMA((6,)),
        ],
    )(mixed, tokens_grad, grads)


def local(split, tokens, frames, g1, b1, wqkv, bqv, wo, bo, g2, b2, w1, b1f, w2, b2f, cotangent):
    spot = lax.axis_index("fsdp") // split

    def block(values):
        if split == 1:
            return values
        n = values.shape[0]
        every = lax.all_gather(values, "fsdp", axis=0, tiled=True)
        return lax.dynamic_slice(every, (spot * split * n,), (split * n,))

    def owned(values):
        if split == 1:
            return values
        n = values.shape[0]
        spread = lax.dynamic_update_slice(jnp.zeros((8 * n,), F32), values, (spot * n,))
        return lax.psum_scatter(spread, "fsdp", scatter_dimension=0, tiled=True)

    small = [block(v).reshape(1, -1) for v in (g1, b1, bqv, bo, g2, b2, b1f, b2f)]
    shards = [block(v).reshape(-1, 128) for v in (wqkv, wo, w1, w2)]
    outs = hand_out(*call_layer(split, tokens, frames.reshape(1, -1), small, shards, cotangent))
    mixed, tokens_grad = outs[:2]
    dg1, db1, dbqv, dbo, dg2, db2, db1f, db2f = [owned(v.reshape(-1)) for v in outs[2:10]]
    dwqkv, dwo, dw1, dw2 = [owned(v.reshape(-1)) for v in outs[10:]]
    return (mixed, tokens_grad, dg1, db1, dwqkv, dbqv, dwo, dbo, dg2, db2, dw1, db1f, dw2, db2f)


def solution(mesh):
    split = mesh.shape["fsdp"] // 8
    flat, rows = P(("dp", "fsdp")), P(("dp", "fsdp"), None)

    def body(*args):
        return local(split, *args)

    return jax.shard_map(
        body,
        mesh=mesh,
        in_specs=(rows,) + (flat,) * 13 + (rows,),
        out_specs=(rows, rows) + (flat,) * 12,
        check_vma=False,
    )
```

time: 130 us -> 93.6 us (0.72)
  Pallas kernels: 118 us -> 92.5 us
  local copies, waits for them, and re-layouts: 10.4 us -> 0 us
    pallas_call x1, Pallas kernels: 118 us -> 89.3 us  [call_layer(): pl.pallas_call(body, name='layer', out_shape=out_shape, in_specs=[any_spe...]
    unnamed x40 -> x0, local copies, waits for them, and re-layouts: 10.4 us -> none
    pallas_call x0 -> x1, Pallas kernels: none -> 3.21 us  [hand_out(): pl.pallas_call(body, name='hand_out', out_shape=row_shapes + small_shapes...]
where the time goes in v2:
time: 93.6 us; the launch traced here: 93.4 us
  Pallas kernels  92.5 us (99%)
    pallas_call x1, Pallas kernels, call_layer(): pl.pallas_call(body, name='layer', out_shape=out_shape, in_specs=[any_spe...  89.3 us
    pallas_call x1, Pallas kernels, hand_out(): pl.pallas_call(body, name='hand_out', out_shape=row_shapes + small_shapes...  3.21 us

profile of v2, /device:TPU:0, one launch (start us, length us, event | category | flops | bytes accessed | tf_op | source)
XLA Modules:
  0.0 93.4 jit_solution(7978098423336831093)
XLA Ops:
  0.7 89.3 %layer.1 = (bf16[960,512]{1,0:T(8,128)(2,1)}, bf16[960,512]{1,0:T(8,128)(2,1)}, f32[776,128]{1,0:T(8,128)}) custom-call(bf16[960,512]{1,0:T(8,128)(2,1)} %refs_0_.1, bf16[960,512]{1,0:T(8,128)(2,1)} %refs_1_.1, s32[1,192]{1,0:T(1,128)} %bitcast.33, f32[1,16]{1,0:T(1,128)} %bitcast.34, f32[1,16]{1,0:T(1,128)} %bitcast.35, f32[1,32]{1,0:T(1,128)} %bitcast.36, ...), custom_call_target="tpu_custom_call" | custom-call | flops 18119393280 | bytes 8388608 | tf_op jit(solution)/shard_map/layer/pallas_call | solution.py:801
  90.0 3.2 %hand_out.1 = (bf16[960,512]{1,0:T(8,128)(2,1)}, bf16[960,512]{1,0:T(8,128)(2,1)}, f32[1,16]{1,0:T(1,128)}, f32[1,16]{1,0:T(1,128)}, f32[1,32]{1,0:T(1,128)}, /*...) custom-call(bf16[960,512]{1,0:T(8,128)(2,1)} %get-tuple-element.31.m, ...), custom_call_target="tpu_custom_call" | custom-call | tf_op jit(solution)/shard_map/hand_out/pallas_call | solution.py:844

commit v3 on v2

--- a/solution.py
+++ b/solution.py
@@ -23,8 +23,9 @@
 ROWS = (8, 16, 16, 16, 16, 64)
 COLS = (128, 3 * D // 2, 3 * D // 2, D, FF, D)
 KEPT = (F32, BF16, BF16, BF16, BF16, BF16)
-DIRECT = (SM, QA, QB)
+DIRECT = (SM, QA, QB,)
 HALF = D // 2
+WIDE = FF // 2
 GROUP = HEADS // 2
 QKV_ARG, OUT_ARG, UP_ARG, DOWN_ARG = range(4)
 ARG = (None, QKV_ARG, QKV_ARG, OUT_ARG, UP_ARG, DOWN_ARG)
@@ -72,11 +73,13 @@
         del refs[:n]
         return head
 
-    tok_hbm, cot_hbm, frames_ref = take(3)
-    small_in = take(8)
+    tok_hbm, cot_hbm, frames_hbm = take(3)
+    small_hbm = take(8)
     shard_hbm = take(4)
     mixed_hbm, tgrad_hbm, grads_hbm = take(3)
     shard_in = take(4)
+    small_in = take(8)
+    (frames_in,) = take(1)
     (grads,) = take(1)
     whole = take(6)
     acc = take(6)
@@ -84,9 +87,11 @@
     two_out, two_in = take(6), take(6)
     one_out, one_in = take(6), take(6)
     zed_out, zed_in = take(6), take(6)
-    (tokb, cotb, stage, xt, dm, xh1, xh2, rs1, rs2, a1, a2, qkv, prob, ctx, x1, act, slope, wide, dao, dpre, turned) = take(21)
+    (tokb, cotb, stage, xt, dm, xh1, xh2, rs1, rs2, a1, a2, qkv, prob, ctx, x1, act, slope, wide, dpre, turned) = take(20)
     (vec16, vecqv, vecup, biasq, living, pick, pick_t, gs16, gsqv, gsup, sums) = take(11)
-    (gsend, grecv, rsend, rrecv, io_sem) = take(5)
+    (gsend, grecv, rsend, rrecv, io_sem, small_sem) = take(6)
+
+    dao = cotb
 
     seqs = count // FRAMES
     dp = lax.axis_index("dp")
@@ -115,16 +120,16 @@
     zeds = (z + 1 - 2 * (z % 2), (z + 2) % 4, 3 - z)
     zed_dev = [device(x, c, zk, y) for zk in zeds]
 
-    tok_copy = pltpu.make_async_copy(tok_hbm, tokb, io_sem.at[0])
-    cot_copy = pltpu.make_async_copy(cot_hbm, cotb, io_sem.at[1])
-    shard_copy = [pltpu.make_async_copy(shard_hbm[k], shard_in[k], io_sem.at[4 + k]) for k in range(4)]
-    for copy in shard_copy:
-        copy.start()
-    tok_copy.start()
-    cot_copy.start()
     barrier = pltpu.get_barrier_semaphore()
     for dev in [sibling, first_dev, second_dev, across_dev] + zed_dev:
         pl.semaphore_signal(barrier, inc=1, device_id=dev, device_id_type=MESH)
+    small_copy_in = [pltpu.make_async_copy(small_hbm[p], small_in[p], small_sem.at[p]) for p in range(8)]
+    shard_copy = [pltpu.make_async_copy(shard_hbm[k], shard_in[k], io_sem.at[4 + k]) for k in range(4)]
+    frames_copy = pltpu.make_async_copy(frames_hbm, frames_in, small_sem.at[8])
+    tok_copy = pltpu.make_async_copy(tok_hbm, tokb, io_sem.at[0])
+    cot_copy = pltpu.make_async_copy(cot_hbm, cotb, io_sem.at[1])
+    for copy in small_copy_in + shard_copy + [tok_copy, frames_copy, cot_copy]:
+        copy.start()
 
     def shard(w, f_, s_, z_):
         x_, y_ = to_xy(f_, s_)
@@ -148,6 +153,7 @@
         if w == SM:
             whole[w][x, c, z, y] = jnp.zeros((8, 128), F32)
             for p, n in enumerate(SMALL):
+                small_copy_in[p].wait()
                 whole[w][x, c, z, y, p : p + 1, 0:n] = small_in[p][...].astype(BF16).astype(F32)
         else:
             if w != QB:
@@ -339,8 +345,9 @@
         pick[...] = jnp.where((row // HEAD_DIM == lane % GROUP) & (lane < 2 * GROUP), 1.0, 0.0).astype(BF16)
         lane, row = iota((128, HALF), 1), iota((128, HALF), 0)
         pick_t[...] = jnp.where((lane // HEAD_DIM == row % GROUP) & (row < 2 * GROUP), 1.0, 0.0).astype(BF16)
+        frames_copy.wait()
         same = iota((seqs, seqs), 0) == iota((seqs, seqs), 1)
-        wide_frames = jnp.broadcast_to(frames_ref[...].astype(F32), (seqs, seqs))
+        wide_frames = jnp.broadcast_to(frames_in[...].astype(F32), (seqs, seqs))
         spread = jnp.where(same, wide_frames, 0.0).astype(BF16)
         living[...] = dot(spread, jnp.ones((seqs, 128), BF16))
         gs16[...] = jnp.zeros_like(gs16)
@@ -412,19 +419,15 @@
         return pl.ds(pl.multiple_of(n * width, width), width)
 
     def matrix_cols(w, n, width):
-        part = whole[w][:, :, :, :, :, cols(n, width)]
-        return part.reshape(32 * ROWS[w], width)
+        return whole[w][:, :, :, :, :, cols(n, width)].reshape(32 * ROWS[w], width)
 
     def matrix(w):
         return whole[w][...].reshape(32 * ROWS[w], COLS[w])
 
     def project_in(h):
-        def body(n):
-            at = cols(n + 3 * h, HALF)
-            r = dot(a1[...], matrix_cols(QA + h, n, HALF)) + biasq[:, at]
-            qkv[:, at] = r.astype(BF16)
-
-        loop(3, body)
+        at = slice(3 * HALF * h, 3 * HALF * (h + 1))
+        r = dot(a1[...], matrix(QA + h)) + biasq[:, at]
+        qkv[:, at] = r.astype(BF16)
 
     def frame_rows(t, i):
         return pl.ds(pl.multiple_of(t * seqs + i * CHUNK, CHUNK), CHUNK)
@@ -535,12 +538,12 @@
         k1 = k0 * 0.044715
 
         def body(n):
-            f = dot(a2[...], matrix_cols(UP, n, 256)) + vecup[UPB : UPB + 1, cols(n, 256)]
+            f = dot(a2[...], matrix_cols(UP, n, WIDE)) + vecup[UPB : UPB + 1, cols(n, WIDE)]
             square = f * f
             half = 0.5 + 0.5 * jnp.tanh(f * (k0 + k1 * square))
-            act[:, cols(n, 256)] = (f * half).astype(BF16)
+            act[:, cols(n, WIDE)] = (f * half).astype(BF16)
             grow = half + (f * (half - half * half)) * (2.0 * k0 + 6.0 * k1 * square)
-            slope[:, cols(n, 256)] = grow.astype(BF16)
+            slope[:, cols(n, WIDE)] = grow.astype(BF16)
 
         loop(stop, body, start)
 
@@ -553,28 +556,16 @@
             for h in range(2):
                 stage[2 * n + h, pl.ds(t, seqs, stride=FRAMES), :] = r[t * seqs : (t + 1) * seqs, h * 128 : (h + 1) * 128]
 
-    def turn(left, core):
-        parts = [left[:, pl.ds(pl.multiple_of(h * 256 + core * 128, 128), 128)] for h in range(2)]
+    def turn(left):
+        parts = [left[:, pl.ds(pl.multiple_of(h * 256 + core * 128, 128), 128)] for core in (1 - c, c) for h in range(2)]
         turned[...] = jnp.transpose(jnp.concatenate(parts, axis=1))
 
-    def grad_theirs(w, left, right, base, width):
-        turn(left, 1 - c)
-
-        def body(n):
-            r = dot(turned[...], right[:, cols(n + base, width)])
-            sib_out[w][:, :, cols(n, width)] = r.reshape(16, ROWS[w], width).astype(BF16)
-
-        loop(COLS[w] // width, body)
-        sib_copy(w, 0, 16).start()
-
-    def grad_ours(w, left, right, base, width):
-        turn(left, c)
-
-        def body(n):
-            r = dot(turned[...], right[:, cols(n + base, width)])
-            acc[w][:, :, cols(n, width)] = r.reshape(16, ROWS[w], width)
-
-        loop(COLS[w] // width, body)
+    def weight_grad(w, right, base, n, width):
+        at = slice(n * width, (n + 1) * width)
+        r = dot(turned[...], right[:, base + n * width : base + (n + 1) * width])
+        sib_out[w][:, :, at] = r[:HALF].reshape(16, ROWS[w], width).astype(BF16)
+        rcopy(w, 0, 0, sib_out[w].at[:, :, at], sib_in[w].at[:, :, at], sibling).start()
+        acc[w][:, :, at] = r[HALF:].reshape(16, ROWS[w], width)
 
     def down_theirs(h):
         left = act[:, pl.ds(pl.multiple_of(h * 1024 + (1 - c) * 512, 512), 512)]
@@ -588,10 +579,10 @@
 
     def feed_back(start, stop):
         def body(n):
-            part = whole[DOWN][n // 4, (n // 2) % 2, pl.ds(2 * (n % 2), 2)].reshape(256, D)
-            low = (dot_nt(dm[...], part) * slope[:, cols(n, 256)].astype(F32)).astype(BF16)
-            slope[:, cols(n, 256)] = low
-            gsup[UPB : UPB + 1, cols(n, 256)] = jnp.sum(fold(low.astype(F32)), axis=0, keepdims=True)
+            part = whole[DOWN][n].reshape(WIDE, D)
+            low = (dot_nt(dm[...], part) * slope[:, cols(n, WIDE)].astype(F32)).astype(BF16)
+            slope[:, cols(n, WIDE)] = low
+            gsup[UPB : UPB + 1, cols(n, WIDE)] = jnp.sum(fold(low.astype(F32)), axis=0, keepdims=True)
 
         loop(stop, body, start)
 
@@ -638,120 +629,122 @@
         loop(tiles, body)
         narrow(cotb)
 
-    own_shard(SM)
     own_shard(QA)
     own_shard(QB)
+    own_shard(SM)
+    own_shard(OUT)
+    own_shard(UP)
+    own_shard(DOWN)
     pl.semaphore_wait(barrier, 7)
     g_start(SM)
-    g_start(QA)
-    constants()
+    g_start(OUT)
+    g_start(QB)
+    g_start(UP)
     tok_copy.wait()
     first_norm()
-    own_shard(OUT)
-    g_start(OUT)
-    g_start(QB)
-    own_shard(UP)
-    g_start(UP)
+    g_start(QA)
+    g_start(DOWN)
     g_z(SM)
-    g_z(QA)
     g_z(OUT)
-    own_shard(DOWN)
-    g_start(DOWN)
+    g_z(QB)
     g_s(SM)
     g_sib(SM)
-    g_z(QB)
-    g_s(QA)
-    g_sib(QA)
+    g_f(OUT)
+    small_vectors()
+    constants()
+    g_z(UP)
+    g_s(QB)
     cot_copy.wait()
     cotangent_in()
-    g_f(OUT)
-    g_z(UP)
-    g_s(QB)
-    small_vectors()
+    g_z(QA)
     first_affine()
-    project_in(0)
-    loop(1, lambda i: attention(0, i), 0)
     g_sib(QB)
-    g_f(UP)
     g_s(OUT)
     project_in(1)
+    loop(1, lambda i: attention(1, i), 0)
+    g_f(UP)
+    loop(2, lambda i: attention(1, i), 1)
     g_z(DOWN)
-    loop(3, lambda i: attention(0, i), 1)
-    loop(2, lambda i: attention(1, i), 0)
+    loop(3, lambda i: attention(1, i), 2)
+    g_s(QA)
     g_sib(OUT)
-    loop(3, lambda i: attention(1, i), 2)
+    g_sib(QA)
+    project_in(0)
+    loop(3, lambda i: attention(0, i), 0)
     g_s(UP)
     project_out()
-    second_norm(0, 5)
+    second_norm(0, 2)
     g_f(DOWN)
+    second_norm(2, 5)
     g_sib(UP)
-    feed_up(0, 8)
+    feed_up(0, 2)
+    down_ours(0)
+    g_s(DOWN)
     down_theirs(0)
-    g_s(DOWN)
     down_theirs(1)
-    down_ours(0)
     down_ours(1)
     g_sib(DOWN)
-    feed_back(0, 4)
+    feed_back(0, 2)
     r_1(DOWN)
-    feed_back(4, 8)
+    turn(a2)
+    weight_grad(UP, slope, 0, 0, WIDE)
+    turn(a2)
+    weight_grad(UP, slope, 0, 1, WIDE)
     back_to(slope, UP, 0)
-    grad_theirs(UP, a2, slope, 0, 512)
-    grad_ours(UP, a2, slope, 0, 512)
+    back_to(slope, UP, 1)
     r_2(DOWN)
-    back_to(slope, UP, 1)
+    second_back(0, 5)
     r_1(UP)
-    second_back(0, 5)
     back_to(dao, OUT, 0)
     back_to(dao, OUT, 1)
-    grad_ours(OUT, ctx, dao, 0, 512)
-    loop(1, lambda i: attention_back(1, i), 0)
-    grad_theirs(OUT, ctx, dao, 0, 512)
     loop(2, lambda i: attention_back(0, i), 0)
     r_3(DOWN)
+    turn(ctx)
+    weight_grad(OUT, dao, 0, 0, D)
+    loop(3, lambda i: attention_back(0, i), 2)
+    turn(a1)
+    weight_grad(QA, dpre, 0, 0, 3 * HALF)
+    loop(1, lambda i: attention_back(1, i), 0)
     r_2(UP)
-    loop(3, lambda i: attention_back(0, i), 2)
+    loop(3, lambda i: attention_back(1, i), 1)
+    r_1(QA)
     r_1(OUT)
-    grad_theirs(QA, a1, dpre, 0, HALF)
-    loop(3, lambda i: attention_back(1, i), 1)
-    grad_ours(QA, a1, dpre, 0, HALF)
-    r_1(QA)
-    grad_theirs(QB, a1, dpre, 3, HALF)
+    back_in(0)
+    back_in(1)
+    turn(a1)
+    weight_grad(QB, dpre, 3 * HALF, 0, 3 * HALF)
     r_3(UP)
-    r_2(OUT)
-    grad_ours(QB, a1, dpre, 3, HALF)
-    back_in(0)
-    r_1(QB)
     r_2(QA)
-    back_in(1)
     first_back()
     tgrad_copy = pltpu.make_async_copy(cotb, tgrad_hbm, io_sem.at[3])
     tgrad_copy.start()
+    r_1(QB)
     small_grads()
+    r_3(QA)
+    r_2(OUT)
     r_2(QB)
-    r_3(QA)
+    r_1(SM)
+    feed_down(0)
     r_3(OUT)
-    r_1(SM)
     r_3(QB)
-    r_4(DOWN)
-    arg_copy(DOWN_ARG).start()
     r_2(SM)
     r_3(SM)
-    r_4(UP)
-    arg_copy(UP_ARG).start()
     for w in (SM, QA, QB, OUT, UP, DOWN):
         g_end(w)
     r_4(QA)
-    feed_down(0)
+    r_4(UP)
+    arg_copy(UP_ARG).start()
     feed_down(1)
     narrow(tokb)
     mixed_copy = pltpu.make_async_copy(tokb, mixed_hbm, io_sem.at[2])
     mixed_copy.start()
+    r_4(DOWN)
+    arg_copy(DOWN_ARG).start()
     r_4(OUT)
     arg_copy(OUT_ARG).start()
-    r_4(SM)
     r_4(QB)
     arg_copy(QKV_ARG).start()
+    r_4(SM)
     for w in (SM, QA, QB, OUT, UP, DOWN):
         r_end(w)
     for k in range(4):
@@ -764,12 +757,13 @@
 def call_layer(split, tokens, frames, small, shards, cotangent):
     count = tokens.shape[0]
     any_spec = pl.BlockSpec(memory_space=pl.ANY)
-    vmem = pl.BlockSpec(memory_space=pltpu.VMEM)
 
     def kept(n, dtype=None):
         return [pltpu.VMEM((n, r, k), dtype or t) for r, k, t in zip(ROWS, COLS, KEPT)]
 
-    scratch = [pltpu.VMEM((n, 128), F32) for n in PACKED] + [pltpu.VMEM((PACK_ALL, 128), F32)]
+    scratch = [pltpu.VMEM((n, 128), F32) for n in PACKED]
+    scratch += [pltpu.VMEM((1, n), F32) for n in SMALL] + [pltpu.VMEM((1, count // FRAMES), jnp.int32)]
+    scratch += [pltpu.VMEM((PACK_ALL, 128), F32)]
     scratch += [pltpu.VMEM((2, 2, 4, 2, r, k), t) for r, k, t in zip(ROWS, COLS, KEPT)]
     scratch += kept(16, F32)
     for n in (16, 8, 4, 3):
@@ -782,7 +776,7 @@
         rows_bf(D), rows_bf(D), rows_bf(3 * D),
         pltpu.VMEM((2, len(PAIRS), count // FRAMES, 128), F32),
         rows_bf(D), rows_f(D), rows_bf(FF), rows_bf(FF),
-        rows_f(D), rows_bf(D), rows_bf(3 * D), pltpu.VMEM((HALF, count), BF16),
+        rows_f(D), rows_bf(3 * D), pltpu.VMEM((D, count), BF16),
     ]
     scratch += [
         pltpu.VMEM((8, 512), F32), pltpu.VMEM((8, 1024), F32), pltpu.VMEM((8, 2048), F32), pltpu.VMEM((1, 3 * D), F32),
@@ -791,7 +785,7 @@
         pltpu.VMEM((2, 2, 8, 8, 128), F32),
     ]
     scratch += [pltpu.SemaphoreType.DMA((6, n)) for n in (5, 10, 4, 11)]
-    scratch += [pltpu.SemaphoreType.DMA((13,))]
+    scratch += [pltpu.SemaphoreType.DMA((13,)), pltpu.SemaphoreType.DMA((9,))]
     out_shape = [jax.ShapeDtypeStruct(tokens.shape, BF16)] * 2
     out_shape += [jax.ShapeDtypeStruct((PACK_ALL, 128), F32)]
 
@@ -802,7 +796,7 @@
         body,
         name="layer",
         out_shape=out_shape,
-        in_specs=[any_spec, any_spec] + [vmem] * 9 + [any_spec] * 4,
+        in_specs=[any_spec] * 15,
         out_specs=[any_spec] * 3,
         scratch_shapes=scratch,
         compiler_params=pltpu.CompilerParams(

time: 93.6 us -> 87.9 us (0.939)
  Pallas kernels: 92.5 us -> 86.9 us
    pallas_call x1, Pallas kernels: 89.3 us -> 83.6 us  [call_layer(): pl.pallas_call(body, name='layer', out_shape=out_shape, in_specs=[any_spe...]
where the time goes in v3:
time: 87.9 us; the launch traced here: 87.7 us
  Pallas kernels  86.9 us (99%)
    pallas_call x1, Pallas kernels, call_layer(): pl.pallas_call(body, name='layer', out_shape=out_shape, in_specs=[any_spe...  83.6 us
    pallas_call x1, Pallas kernels, hand_out(): pl.pallas_call(body, name='hand_out', out_shape=row_shapes + small_shapes...  3.21 us

profile of v3, /device:TPU:0, one launch (start us, length us, event | category | flops | bytes accessed | tf_op | source)
XLA Modules:
  0.0 87.7 jit_solution(2549472040203902481)
XLA Ops:
  0.7 83.6 %layer.1 = (bf16[960,512]{1,0:T(8,128)(2,1)}, bf16[960,512]{1,0:T(8,128)(2,1)}, f32[776,128]{1,0:T(8,128)}) custom-call(bf16[960,512]{1,0:T(8,128)(2,1)} %refs_0_.1, bf16[960,512]{1,0:T(8,128)(2,1)} %refs_1_.1, s32[1,192]{1,0:T(1,128)} %bitcast.33, f32[1,16]{1,0:T(1,128)} %bitcast.34, f32[1,16]{1,0:T(1,128)} %bitcast.35, f32[1,32]{1,0:T(1,128)} %bitcast.36, ...), custom_call_target="tpu_custom_call" | custom-call | flops 18119393280 | bytes 8388608 | tf_op jit(solution)/shard_map/layer/pallas_call | solution.py:795
  84.3 3.2 %hand_out.1 = (bf16[960,512]{1,0:T(8,128)(2,1)}, bf16[960,512]{1,0:T(8,128)(2,1)}, f32[1,16]{1,0:T(1,128)}, f32[1,16]{1,0:T(1,128)}, f32[1,32]{1,0:T(1,128)}, /*...) custom-call(bf16[960,512]{1,0:T(8,128)(2,1)} %get-tuple-element.31.m, ...), custom_call_target="tpu_custom_call" | custom-call | tf_op jit(solution)/shard_map/hand_out/pallas_call | solution.py:838

commit v4 on v3

--- a/solution.py
+++ b/solution.py
@@ -100,18 +100,23 @@
     group, rest = fs // split, fs % split
     z, y = group // 2, group % 2
 
+    plane = (c + x + y) % 2
+
+    def core_at(x_, y_):
+        return (plane + x_ + y_) % 2
+
     def device(x_, c_, z_, y_):
         return (x_ * 2 + c_, (z_ * 2 + y_) * split + rest)
 
-    first = x + c * (y - x)
-    second = y + c * (x - y)
+    first = x + plane * (y - x)
+    second = y + plane * (x - y)
 
     def to_xy(f_, s_):
-        return f_ + c * (s_ - f_), s_ + c * (f_ - s_)
+        return f_ + plane * (s_ - f_), s_ + plane * (f_ - s_)
 
     def peer(f_, s_):
         x_, y_ = to_xy(f_, s_)
-        return device(x_, c, z, y_)
+        return device(x_, core_at(x_, y_), z, y_)
 
     sibling = device(x, 1 - c, z, y)
     first_dev = peer(1 - first, second)
@@ -133,11 +138,11 @@
 
     def shard(w, f_, s_, z_):
         x_, y_ = to_xy(f_, s_)
-        return whole[w].at[x_, c, z_, y_]
+        return whole[w].at[x_, core_at(x_, y_), z_, y_]
 
     def line(w, f_, s_):
         x_, y_ = to_xy(f_, s_)
-        return whole[w].at[x_, c, :, y_]
+        return whole[w].at[x_, core_at(x_, y_), :, y_]
 
     def gcopy(w, sent, got, ref, dev):
         return pltpu.make_async_remote_copy(
@@ -247,12 +252,24 @@
     def zed_copy(w, k):
         return rcopy(w, 3, 10, zed_out[w].at[k], zed_in[w].at[k], zed_dev[k])
 
+    def chip_sum(w, j):
+        return acc[w][j] + sib_in[w][j].astype(F32)
+
     def r_1(w):
         sib_copy(w, 0, 16).wait_recv()
+        if w == SM:
+            for k in range(4):
+                one_out[w][k] = chip_sum(w, place(1 - first, second, k))
+                rcopy(w, 2, 6, one_out[w].at[k], one_in[w].at[k], first_dev).start()
+                two_out[w][k] = chip_sum(w, place(first, 1 - second, k))
+                two_copy(w, k, 5).start()
+                two_out[w][4 + k] = chip_sum(w, place(1 - first, 1 - second, k))
+                rcopy(w, 1, 1, two_out[w].at[4 + k], two_in[w].at[4 + k], across_dev).start()
+            return
 
         def step(k, got):
             j = place(k // 4, 1 - second, k % 4)
-            two_out[w][k] = (acc[w][j] + sib_in[w][j].astype(F32)).astype(KEPT[w])
+            two_out[w][k] = chip_sum(w, j).astype(KEPT[w])
             two_copy(w, k, got).start()
 
         loop(4, lambda i: step(4 * (1 - first) + i, 1 + i))
@@ -264,21 +281,32 @@
             j = place(1 - first, second, k)
             slot = (1 - first) * 4 + k
             two_copy(w, slot, 1 + k).wait_recv()
-            total = acc[w][j] + sib_in[w][j].astype(F32) + two_in[w][slot].astype(F32)
+            total = chip_sum(w, j) + two_in[w][slot].astype(F32)
             one_out[w][k] = total.astype(KEPT[w])
             one_copy(w, k).start()
 
         loop(4, step)
 
+    def line_sum(w, k):
+        j = place(first, second, k)
+        total = chip_sum(w, j) + one_in[w][k].astype(F32)
+        if w == SM:
+            return total + two_in[w][k] + two_in[w][4 + k]
+        return total + two_in[w][4 * first + k].astype(F32)
+
     def r_3(w):
-        line_in = two_in[w].at[pl.ds(4 * first, 4)]
-        rcopy(w, 1, 5, line_in, line_in, second_dev).wait_recv()
+        if w == SM:
+            rcopy(w, 2, 6, one_in[w], one_in[w], first_dev).wait_recv()
+            for got, at in ((5, 0), (1, 4)):
+                part = two_in[w].at[pl.ds(at, 4)]
+                rcopy(w, 1, got, part, part, second_dev).wait_recv()
+        else:
+            line_in = two_in[w].at[pl.ds(4 * first, 4)]
+            rcopy(w, 1, 5, line_in, line_in, second_dev).wait_recv()
         for k in range(3):
-            j = place(first, second, zeds[k])
-            slot = first * 4 + zeds[k]
-            one_copy(w, zeds[k]).wait_recv()
-            total = acc[w][j] + sib_in[w][j].astype(F32) + two_in[w][slot].astype(F32) + one_in[w][zeds[k]].astype(F32)
-            zed_out[w][k] = total.astype(KEPT[w])
+            if w != SM:
+                one_copy(w, zeds[k]).wait_recv()
+            zed_out[w][k] = line_sum(w, zeds[k]).astype(KEPT[w])
             zed_copy(w, k).start()
 
     def grad_copy(at, rows, k):
@@ -290,10 +318,9 @@
     small_copy = grad_copy(PACK_SMALL, 8, 4)
 
     def r_4(w):
-        j = place(first, second, z)
-        slot = first * 4 + z
-        one_copy(w, z).wait_recv()
-        total = acc[w][j] + sib_in[w][j].astype(F32) + two_in[w][slot].astype(F32) + one_in[w][z].astype(F32)
+        if w != SM:
+            one_copy(w, z).wait_recv()
+        total = line_sum(w, z)
         rcopy(w, 3, 10, zed_in[w], zed_in[w], sibling).wait_recv()
         for k in range(3):
             total = total + zed_in[w][k].astype(F32)
@@ -401,10 +428,13 @@
                 near = jnp.where(iota((128, 512), 0) == (iota((128, 512), 1) + at) % n, 1.0, 0.0).astype(BF16)
                 part = dot_nt(high, near) + dot_nt(low, near)
                 total = part if n == 16 and at == 0 else total + part
-        sums[...] = total.reshape(2, 2, 8, 8, 128)
+        sums[...] = total.reshape(2, 2, 4, 2, 8, 128)
         for h in range(2):
-            acc[SM][8 * h : 8 * h + 8] = sums[h, c]
-            sib_out[SM][8 * h : 8 * h + 8] = sums[h, 1 - c]
+            for q in range(2):
+                for own in range(2):
+                    part = sums[h, core_at(h, q) if own else 1 - core_at(h, q), :, q]
+                    for k in range(4):
+                        (acc if own else sib_out)[SM][8 * h + 2 * k + q] = part[k]
             sib_copy(SM, 8 * h, 8).start()
 
     def first_affine():
@@ -557,25 +587,33 @@
                 stage[2 * n + h, pl.ds(t, seqs, stride=FRAMES), :] = r[t * seqs : (t + 1) * seqs, h * 128 : (h + 1) * 128]
 
     def turn(left):
-        parts = [left[:, pl.ds(pl.multiple_of(h * 256 + core * 128, 128), 128)] for core in (1 - c, c) for h in range(2)]
-        turned[...] = jnp.transpose(jnp.concatenate(parts, axis=1))
+        for h in range(2):
+            for k in range(2):
+                at = h * 256 + k * 128
+                part = jnp.transpose(left[:, at : at + 128]).reshape(4, 2, 16, count)
+                for q in range(2):
+                    turned[(k + core_at(h, q) + 1) % 2, h, :, q] = part[:, q]
 
     def weight_grad(w, right, base, n, width):
         at = slice(n * width, (n + 1) * width)
-        r = dot(turned[...], right[:, base + n * width : base + (n + 1) * width])
+        r = dot(turned[...].reshape(D, count), right[:, base + n * width : base + (n + 1) * width])
         sib_out[w][:, :, at] = r[:HALF].reshape(16, ROWS[w], width).astype(BF16)
         rcopy(w, 0, 0, sib_out[w].at[:, :, at], sib_in[w].at[:, :, at], sibling).start()
         acc[w][:, :, at] = r[HALF:].reshape(16, ROWS[w], width)
 
+    def act_of(h, own):
+        core = core_at(h, 0) if own else 1 - core_at(h, 0)
+        even = act[:, pl.ds(pl.multiple_of(h * 1024 + core * 512, 512), 512)]
+        odd = act[:, pl.ds(pl.multiple_of(h * 1024 + (1 - core) * 512, 512), 512)]
+        return jnp.where(iota((count, 512), 1) % 128 < 64, even, odd)
+
     def down_theirs(h):
-        left = act[:, pl.ds(pl.multiple_of(h * 1024 + (1 - c) * 512, 512), 512)]
-        r = dot_tn(left, dm[...])
+        r = dot_tn(act_of(h, False), dm[...])
         sib_out[DOWN][8 * h : 8 * h + 8] = r.reshape(8, 64, D).astype(BF16)
         sib_copy(DOWN, 8 * h, 8).start()
 
     def down_ours(h):
-        left = act[:, pl.ds(pl.multiple_of(h * 1024 + c * 512, 512), 512)]
-        acc[DOWN][8 * h : 8 * h + 8] = dot_tn(left, dm[...]).reshape(8, 64, D)
+        acc[DOWN][8 * h : 8 * h + 8] = dot_tn(act_of(h, True), dm[...]).reshape(8, 64, D)
 
     def feed_back(start, stop):
         def body(n):
@@ -643,105 +681,103 @@
     tok_copy.wait()
     first_norm()
     g_start(QA)
+    constants()
     g_start(DOWN)
-    g_z(SM)
     g_z(OUT)
     g_z(QB)
-    g_s(SM)
-    g_sib(SM)
-    g_f(OUT)
-    small_vectors()
-    constants()
+    g_z(SM)
     g_z(UP)
     g_s(QB)
+    g_s(SM)
     cot_copy.wait()
     cotangent_in()
     g_z(QA)
+    g_sib(SM)
+    small_vectors()
+    g_sib(QB)
+    g_f(OUT)
     first_affine()
-    g_sib(QB)
-    g_s(OUT)
+    g_f(UP)
     project_in(1)
-    loop(1, lambda i: attention(1, i), 0)
-    g_f(UP)
-    loop(2, lambda i: attention(1, i), 1)
+    loop(2, lambda i: attention(1, i), 0)
+    g_s(QA)
     g_z(DOWN)
     loop(3, lambda i: attention(1, i), 2)
-    g_s(QA)
-    g_sib(OUT)
+    g_s(OUT)
     g_sib(QA)
     project_in(0)
     loop(3, lambda i: attention(0, i), 0)
     g_s(UP)
+    g_sib(OUT)
     project_out()
-    second_norm(0, 2)
+    second_norm(0, 5)
     g_f(DOWN)
-    second_norm(2, 5)
     g_sib(UP)
-    feed_up(0, 2)
+    feed_up(0, 1)
     down_ours(0)
+    down_theirs(0)
+    feed_up(1, 2)
     g_s(DOWN)
-    down_theirs(0)
     down_theirs(1)
     down_ours(1)
     g_sib(DOWN)
-    feed_back(0, 2)
+    feed_back(0, 1)
     r_1(DOWN)
+    feed_back(1, 2)
     turn(a2)
     weight_grad(UP, slope, 0, 0, WIDE)
     turn(a2)
     weight_grad(UP, slope, 0, 1, WIDE)
+    r_2(DOWN)
     back_to(slope, UP, 0)
     back_to(slope, UP, 1)
-    r_2(DOWN)
-    second_back(0, 5)
+    second_back(0, 2)
     r_1(UP)
+    second_back(2, 5)
     back_to(dao, OUT, 0)
     back_to(dao, OUT, 1)
-    loop(2, lambda i: attention_back(0, i), 0)
+    loop(3, lambda i: attention_back(0, i), 0)
+    turn(a1)
+    weight_grad(QA, dpre, 0, 0, 3 * HALF)
     r_3(DOWN)
+    r_2(UP)
+    loop(3, lambda i: attention_back(1, i), 0)
+    r_1(QA)
     turn(ctx)
     weight_grad(OUT, dao, 0, 0, D)
-    loop(3, lambda i: attention_back(0, i), 2)
     turn(a1)
-    weight_grad(QA, dpre, 0, 0, 3 * HALF)
-    loop(1, lambda i: attention_back(1, i), 0)
-    r_2(UP)
-    loop(3, lambda i: attention_back(1, i), 1)
-    r_1(QA)
+    weight_grad(QB, dpre, 3 * HALF, 0, 3 * HALF)
+    r_3(UP)
     r_1(OUT)
     back_in(0)
     back_in(1)
-    turn(a1)
-    weight_grad(QB, dpre, 3 * HALF, 0, 3 * HALF)
-    r_3(UP)
     r_2(QA)
+    r_1(QB)
     first_back()
     tgrad_copy = pltpu.make_async_copy(cotb, tgrad_hbm, io_sem.at[3])
     tgrad_copy.start()
-    r_1(QB)
+    r_2(OUT)
     small_grads()
     r_3(QA)
-    r_2(OUT)
     r_2(QB)
     r_1(SM)
-    feed_down(0)
     r_3(OUT)
     r_3(QB)
-    r_2(SM)
     r_3(SM)
+    r_4(DOWN)
+    arg_copy(DOWN_ARG).start()
+    feed_down(0)
     for w in (SM, QA, QB, OUT, UP, DOWN):
         g_end(w)
     r_4(QA)
     r_4(UP)
     arg_copy(UP_ARG).start()
+    r_4(OUT)
+    arg_copy(OUT_ARG).start()
     feed_down(1)
     narrow(tokb)
     mixed_copy = pltpu.make_async_copy(tokb, mixed_hbm, io_sem.at[2])
     mixed_copy.start()
-    r_4(DOWN)
-    arg_copy(DOWN_ARG).start()
-    r_4(OUT)
-    arg_copy(OUT_ARG).start()
     r_4(QB)
     arg_copy(QKV_ARG).start()
     r_4(SM)
@@ -776,13 +812,13 @@
         rows_bf(D), rows_bf(D), rows_bf(3 * D),
         pltpu.VMEM((2, len(PAIRS), count // FRAMES, 128), F32),
         rows_bf(D), rows_f(D), rows_bf(FF), rows_bf(FF),
-        rows_f(D), rows_bf(3 * D), pltpu.VMEM((D, count), BF16),
+        rows_f(D), rows_bf(3 * D), pltpu.VMEM((2, 2, 4, 2, 16, count), BF16),
     ]
     scratch += [
         pltpu.VMEM((8, 512), F32), pltpu.VMEM((8, 1024), F32), pltpu.VMEM((8, 2048), F32), pltpu.VMEM((1, 3 * D), F32),
         pltpu.VMEM((count // FRAMES, 128), F32), pltpu.VMEM((HALF, 128), BF16), pltpu.VMEM((128, HALF), BF16),
         pltpu.VMEM((8, 512), F32), pltpu.VMEM((8, 1024), F32), pltpu.VMEM((8, 2048), F32),
-        pltpu.VMEM((2, 2, 8, 8, 128), F32),
+        pltpu.VMEM((2, 2, 4, 2, 8, 128), F32),
     ]
     scratch += [pltpu.SemaphoreType.DMA((6, n)) for n in (5, 10, 4, 11)]
     scratch += [pltpu.SemaphoreType.DMA((13,)), pltpu.SemaphoreType.DMA((9,))]
@@ -810,25 +846,28 @@
 
 def hand_out(mixed, tokens_grad, grads):
     any_spec = pl.BlockSpec(memory_space=pl.ANY)
-    vmem = pl.BlockSpec(memory_space=pltpu.VMEM)
 
     def body(mixed_in, tgrad_in, grads_in, *refs):
-        outs, (mixed_v, tgrad_v, grads_v, in_sem, out_sem) = refs[:14], refs[14:]
-        smalls, big = outs[2:10], (outs[0], outs[1]) + tuple(outs[10:])
+        outs, smalls, (mixed_v, tgrad_v, grads_v, in_sem, out_sem) = refs[:14], refs[14:22], refs[22:]
+        big = (outs[0], outs[1]) + tuple(outs[10:])
         reads = [
             pltpu.make_async_copy(src, dst, in_sem.at[k])
             for k, (src, dst) in enumerate(((mixed_in, mixed_v), (tgrad_in, tgrad_v), (grads_in, grads_v)))
         ]
         parts = [mixed_v, tgrad_v] + [grads_v.at[pl.ds(PACK[k], PACKED[k])] for k in range(4)]
         writes = [pltpu.make_async_copy(src, dst, out_sem.at[k]) for k, (src, dst) in enumerate(zip(parts, big))]
-        for copy in reads:
+        for k in (2, 0, 1):
+            reads[k].start()
+        reads[2].wait()
+        for copy in writes[2:]:
             copy.start()
-        for k in range(3):
-            reads[k].wait()
-            for copy in writes[2:] if k == 2 else writes[k : k + 1]:
-                copy.start()
         for p, n in enumerate(SMALL):
             smalls[p][...] = grads_v[PACK_SMALL + p : PACK_SMALL + p + 1, 0:n]
+            writes.append(pltpu.make_async_copy(smalls[p], outs[2 + p], out_sem.at[6 + p]))
+            writes[-1].start()
+        for k in range(2):
+            reads[k].wait()
+            writes[k].start()
         for copy in writes:
             copy.wait()
 
@@ -840,10 +879,11 @@
         name="hand_out",
         out_shape=row_shapes + small_shapes + shard_shapes,
         in_specs=[any_spec] * 3,
-        out_specs=[any_spec] * 2 + [vmem] * 8 + [any_spec] * 4,
-        scratch_shapes=[
+        out_specs=[any_spec] * 14,
+        scratch_shapes=[pltpu.VMEM((1, n), F32) for n in SMALL]
+        + [
             pltpu.VMEM(mixed.shape, BF16), pltpu.VMEM(mixed.shape, BF16), pltpu.VMEM(grads.shape, F32),
-            pltpu.SemaphoreType.DMA((3,)), pltpu.SemaphoreType.DMA((6,)),
+            pltpu.SemaphoreType.DMA((3,)), pltpu.SemaphoreType.DMA((14,)),
         ],
     )(mixed, tokens_grad, grads)
 

time: 87.9 us -> 84.4 us (0.960)
  Pallas kernels: 86.9 us -> 83.4 us
    pallas_call x1, Pallas kernels: 83.6 us -> 80.6 us  [call_layer(): pl.pallas_call(body, name='layer', out_shape=out_shape, in_specs=[any_spe...]
where the time goes in v4:
time: 84.4 us; the launch traced here: 84.2 us
  Pallas kernels  83.4 us (99%)
    pallas_call x1, Pallas kernels, call_layer(): pl.pallas_call(body, name='layer', out_shape=out_shape, in_specs=[any_spe...  80.6 us
    pallas_call x1, Pallas kernels, hand_out(): pl.pallas_call(body, name='hand_out', out_shape=row_shapes + small_shapes...  2.77 us

profile of v4, /device:TPU:0, one launch (start us, length us, event | category | flops | bytes accessed | tf_op | source)
XLA Modules:
  0.0 84.2 jit_solution(11368855185848328219)
XLA Ops:
  0.7 80.6 %layer.1 = (bf16[960,512]{1,0:T(8,128)(2,1)}, bf16[960,512]{1,0:T(8,128)(2,1)}, f32[776,128]{1,0:T(8,128)}) custom-call(bf16[960,512]{1,0:T(8,128)(2,1)} %refs_0_.1, bf16[960,512]{1,0:T(8,128)(2,1)} %refs_1_.1, s32[1,192]{1,0:T(1,128)} %bitcast.33, f32[1,16]{1,0:T(1,128)} %bitcast.34, f32[1,16]{1,0:T(1,128)} %bitcast.35, f32[1,32]{1,0:T(1,128)} %bitcast.36, ...), custom_call_target="tpu_custom_call" | custom-call | flops 18119393280 | bytes 8388608 | tf_op jit(solution)/shard_map/layer/pallas_call | solution.py:831
  81.3 2.8 %hand_out.1 = (bf16[960,512]{1,0:T(8,128)(2,1)}, bf16[960,512]{1,0:T(8,128)(2,1)}, f32[1,16]{1,0:T(1,128)}, f32[1,16]{1,0:T(1,128)}, f32[1,32]{1,0:T(1,128)}, /*...) custom-call(bf16[960,512]{1,0:T(8,128)(2,1)} %get-tuple-element.31.m, ...), custom_call_target="tpu_custom_call" | custom-call | tf_op jit(solution)/shard_map/hand_out/pallas_call | solution.py:877

commit v5 on v4

--- a/solution.py
+++ b/solution.py
@@ -24,6 +24,7 @@
 COLS = (128, 3 * D // 2, 3 * D // 2, D, FF, D)
 KEPT = (F32, BF16, BF16, BF16, BF16, BF16)
 DIRECT = (SM, QA, QB,)
+LARGE = (UP, DOWN)
 HALF = D // 2
 WIDE = FF // 2
 GROUP = HEADS // 2
@@ -89,7 +90,7 @@
     zed_out, zed_in = take(6), take(6)
     (tokb, cotb, stage, xt, dm, xh1, xh2, rs1, rs2, a1, a2, qkv, prob, ctx, x1, act, slope, wide, dpre, turned) = take(20)
     (vec16, vecqv, vecup, biasq, living, pick, pick_t, gs16, gsqv, gsup, sums) = take(11)
-    (gsend, grecv, rsend, rrecv, io_sem, small_sem) = take(6)
+    (gsend, grecv, grecv_large, rsend, rrecv, rrecv_large, io_sem, small_sem) = take(8)
 
     dao = cotb
 
@@ -145,8 +146,10 @@
         return whole[w].at[x_, core_at(x_, y_), :, y_]
 
     def gcopy(w, sent, got, ref, dev):
+        sent_sem = gsend.at[w, sent]
+        got_sem = grecv_large.at[w - UP, got] if w in LARGE else grecv.at[w, got]
         return pltpu.make_async_remote_copy(
-            src_ref=ref, dst_ref=ref, send_sem=gsend.at[w, sent], recv_sem=grecv.at[w, got], device_id=dev, device_id_type=MESH
+            src_ref=ref, dst_ref=ref, send_sem=sent_sem, recv_sem=got_sem, device_id=dev, device_id_type=MESH
         )
 
     def cols_of(w):
@@ -168,17 +171,20 @@
                 part = shard_in[ARG[w]][pl.ds(k, ROWS[w], stride=step), :]
                 whole[w][x, c, z, y, :, to * 128 : (to + 1) * 128] = part.astype(BF16)
 
+    def got_first(w, spot):
+        return 6 + spot if w in LARGE else 3
+
+    def got_sibling(w):
+        return 10 if w in LARGE else 6
+
     def hand_on(w, ref, spot):
+        gcopy(w, 0, got_first(w, spot), ref, first_dev).start()
+        gcopy(w, 0, 4, ref, second_dev).start()
         if w in DIRECT:
-            gcopy(w, 1, 3, ref, first_dev).start()
-            gcopy(w, 2, 7, ref, second_dev).start()
-            gcopy(w, 3, 8, ref, across_dev).start()
-        else:
-            gcopy(w, 1, 3 + spot, ref, first_dev).start()
-            gcopy(w, 2, 7, ref, second_dev).start()
+            gcopy(w, 0, 5, ref, across_dev).start()
 
     def to_sibling(w, f_, s_):
-        gcopy(w, 4, 9, line(w, f_, s_), sibling).start()
+        gcopy(w, 1, got_sibling(w), line(w, f_, s_), sibling).start()
 
     def g_start(w):
         ref = shard(w, first, second, z)
@@ -194,35 +200,30 @@
         to_sibling(w, first, second)
 
     def g_f(w):
+        if w not in LARGE:
+            gcopy(w, 0, 3, line(w, 1 - first, second), first_dev).wait_recv()
         for k in range(4):
             ref = shard(w, 1 - first, second, k)
-            gcopy(w, 1, 3 + k, ref, first_dev).wait_recv()
-            gcopy(w, 2, 8, ref, second_dev).start()
+            if w in LARGE:
+                gcopy(w, 0, 6 + k, ref, first_dev).wait_recv()
+            gcopy(w, 0, 5, ref, second_dev).start()
         to_sibling(w, 1 - first, second)
 
     def g_s(w):
         if w in DIRECT:
-            gcopy(w, 1, 3, line(w, 1 - first, second), first_dev).wait_recv()
+            gcopy(w, 0, 3, line(w, 1 - first, second), first_dev).wait_recv()
             to_sibling(w, 1 - first, second)
-        gcopy(w, 2, 7, line(w, first, 1 - second), second_dev).wait_recv()
+        gcopy(w, 0, 4, line(w, first, 1 - second), second_dev).wait_recv()
         to_sibling(w, first, 1 - second)
-        gcopy(w, 2, 8, line(w, 1 - first, 1 - second), second_dev).wait_recv()
+        gcopy(w, 0, 5, line(w, 1 - first, 1 - second), second_dev).wait_recv()
         to_sibling(w, 1 - first, 1 - second)
 
     def g_sib(w):
-        ref = whole[w].at[:, 1 - c]
-        gcopy(w, 4, 9, ref, sibling).wait_recv()
+        gcopy(w, 1, got_sibling(w), whole[w].at[:, 1 - c], sibling).wait_recv()
 
     def g_end(w):
-        gcopy(w, 0, 0, zed_out[w], sibling).wait_send()
-        four = line(w, first, second)
-        gcopy(w, 1, 3, four, sibling).wait_send()
-        if w in DIRECT:
-            gcopy(w, 2, 7, four, sibling).wait_send()
-            gcopy(w, 3, 8, four, sibling).wait_send()
-        else:
-            gcopy(w, 2, 7, two_out[w], sibling).wait_send()
-        gcopy(w, 4, 9, sib_out[w], sibling).wait_send()
+        gcopy(w, 0, 0, sib_out[w].at[pl.ds(0, 15)], sibling).wait_send()
+        gcopy(w, 1, 0, sib_out[w], sibling).wait_send()
 
     def loop(n, body, start=0):
         def step(i, carry):
@@ -236,21 +237,26 @@
         return x_ * 8 + z_ * 2 + y_
 
     def rcopy(w, sent, got, src, dst, dev):
+        sent_sem = rsend.at[w, sent]
+        got_sem = rrecv_large.at[w - UP, got] if w in LARGE else rrecv.at[w, got]
         return pltpu.make_async_remote_copy(
-            src_ref=src, dst_ref=dst, send_sem=rsend.at[w, sent], recv_sem=rrecv.at[w, got], device_id=dev, device_id_type=MESH
+            src_ref=src, dst_ref=dst, send_sem=sent_sem, recv_sem=got_sem, device_id=dev, device_id_type=MESH
         )
 
     def sib_copy(w, at, n):
-        return rcopy(w, 0, 0, sib_out[w].at[pl.ds(at, n)], sib_in[w].at[pl.ds(at, n)], sibling)
+        return rcopy(w, 1, 0, sib_out[w].at[pl.ds(at, n)], sib_in[w].at[pl.ds(at, n)], sibling)
 
     def two_copy(w, k, got):
-        return rcopy(w, 1, got, two_out[w].at[k], two_in[w].at[k], second_dev)
+        return rcopy(w, 0, got, two_out[w].at[k], two_in[w].at[k], second_dev)
 
     def one_copy(w, k):
-        return rcopy(w, 2, 6 + k, one_out[w].at[k], one_in[w].at[k], first_dev)
+        return rcopy(w, 0, 9 + k if w in LARGE else 3, one_out[w].at[k], one_in[w].at[k], first_dev)
 
     def zed_copy(w, k):
-        return rcopy(w, 3, 10, zed_out[w].at[k], zed_in[w].at[k], zed_dev[k])
+        return rcopy(w, 0, 4, zed_out[w].at[k], zed_in[w].at[k], zed_dev[k])
+
+    def four_of(w, at):
+        return two_in[w].at[pl.ds(at, 4)]
 
     def chip_sum(w, j):
         return acc[w][j] + sib_in[w][j].astype(F32)
@@ -260,11 +266,11 @@
         if w == SM:
             for k in range(4):
                 one_out[w][k] = chip_sum(w, place(1 - first, second, k))
-                rcopy(w, 2, 6, one_out[w].at[k], one_in[w].at[k], first_dev).start()
+                one_copy(w, k).start()
                 two_out[w][k] = chip_sum(w, place(first, 1 - second, k))
-                two_copy(w, k, 5).start()
+                two_copy(w, k, 2).start()
                 two_out[w][4 + k] = chip_sum(w, place(1 - first, 1 - second, k))
-                rcopy(w, 1, 1, two_out[w].at[4 + k], two_in[w].at[4 + k], across_dev).start()
+                rcopy(w, 0, 1, two_out[w].at[4 + k], two_in[w].at[4 + k], across_dev).start()
             return
 
         def step(k, got):
@@ -272,15 +278,20 @@
             two_out[w][k] = chip_sum(w, j).astype(KEPT[w])
             two_copy(w, k, got).start()
 
-        loop(4, lambda i: step(4 * (1 - first) + i, 1 + i))
-        loop(4, lambda i: step(4 * first + i, 5))
+        loop(4, lambda i: step(4 * (1 - first) + i, 5 + i if w in LARGE else 1))
+        loop(4, lambda i: step(4 * first + i, 2))
 
     def r_2(w):
+        if w not in LARGE:
+            part = four_of(w, 4 * (1 - first))
+            rcopy(w, 0, 1, part, part, second_dev).wait_recv()
+
         def step(i):
             k = (z + 1 + i) % 4
             j = place(1 - first, second, k)
             slot = (1 - first) * 4 + k
-            two_copy(w, slot, 1 + k).wait_recv()
+            if w in LARGE:
+                two_copy(w, slot, 5 + k).wait_recv()
             total = chip_sum(w, j) + two_in[w][slot].astype(F32)
             one_out[w][k] = total.astype(KEPT[w])
             one_copy(w, k).start()
@@ -296,15 +307,16 @@
 
     def r_3(w):
         if w == SM:
-            rcopy(w, 2, 6, one_in[w], one_in[w], first_dev).wait_recv()
-            for got, at in ((5, 0), (1, 4)):
-                part = two_in[w].at[pl.ds(at, 4)]
-                rcopy(w, 1, got, part, part, second_dev).wait_recv()
+            waits = ((2, 0), (1, 4))
         else:
-            line_in = two_in[w].at[pl.ds(4 * first, 4)]
-            rcopy(w, 1, 5, line_in, line_in, second_dev).wait_recv()
+            waits = ((2, 4 * first),)
+        for got, at in waits:
+            part = four_of(w, at)
+            rcopy(w, 0, got, part, part, second_dev).wait_recv()
+        if w not in LARGE:
+            rcopy(w, 0, 3, one_in[w], one_in[w], first_dev).wait_recv()
         for k in range(3):
-            if w != SM:
+            if w in LARGE:
                 one_copy(w, zeds[k]).wait_recv()
             zed_out[w][k] = line_sum(w, zeds[k]).astype(KEPT[w])
             zed_copy(w, k).start()
@@ -318,10 +330,10 @@
     small_copy = grad_copy(PACK_SMALL, 8, 4)
 
     def r_4(w):
-        if w != SM:
+        if w in LARGE:
             one_copy(w, z).wait_recv()
         total = line_sum(w, z)
-        rcopy(w, 3, 10, zed_in[w], zed_in[w], sibling).wait_recv()
+        rcopy(w, 0, 4, zed_in[w], zed_in[w], sibling).wait_recv()
         for k in range(3):
             total = total + zed_in[w][k].astype(F32)
         if w == SM:
@@ -334,9 +346,7 @@
 
     def r_end(w):
         sib_copy(w, 0, 16).wait_send()
-        rcopy(w, 1, 5, two_out[w], two_in[w], sibling).wait_send()
-        rcopy(w, 2, 6, one_out[w], one_in[w], sibling).wait_send()
-        rcopy(w, 3, 10, zed_out[w], zed_in[w], sibling).wait_send()
+        rcopy(w, 0, 0, sib_out[w].at[pl.ds(0, 15)], sib_in[w].at[pl.ds(0, 15)], sibling).wait_send()
 
     tiles = count // TILE
     per_frame = seqs // TILE
@@ -598,7 +608,7 @@
         at = slice(n * width, (n + 1) * width)
         r = dot(turned[...].reshape(D, count), right[:, base + n * width : base + (n + 1) * width])
         sib_out[w][:, :, at] = r[:HALF].reshape(16, ROWS[w], width).astype(BF16)
-        rcopy(w, 0, 0, sib_out[w].at[:, :, at], sib_in[w].at[:, :, at], sibling).start()
+        rcopy(w, 1, 0, sib_out[w].at[:, :, at], sib_in[w].at[:, :, at], sibling).start()
         acc[w][:, :, at] = r[HALF:].reshape(16, ROWS[w], width)
 
     def act_of(h, own):
@@ -780,9 +790,9 @@
     mixed_copy.start()
     r_4(QB)
     arg_copy(QKV_ARG).start()
-    r_4(SM)
     for w in (SM, QA, QB, OUT, UP, DOWN):
         r_end(w)
+    r_4(SM)
     for k in range(4):
         arg_copy(k).wait()
     small_copy.wait()
@@ -820,7 +830,7 @@
         pltpu.VMEM((8, 512), F32), pltpu.VMEM((8, 1024), F32), pltpu.VMEM((8, 2048), F32),
         pltpu.VMEM((2, 2, 4, 2, 8, 128), F32),
     ]
-    scratch += [pltpu.SemaphoreType.DMA((6, n)) for n in (5, 10, 4, 11)]
+    scratch += [pltpu.SemaphoreType.DMA(shape) for shape in ((6, 2), (4, 7), (2, 11), (6, 2), (4, 5), (2, 13))]
     scratch += [pltpu.SemaphoreType.DMA((13,)), pltpu.SemaphoreType.DMA((9,))]
     out_shape = [jax.ShapeDtypeStruct(tokens.shape, BF16)] * 2
     out_shape += [jax.ShapeDtypeStruct((PACK_ALL, 128), F32)]

time: 84.4 us -> 84 us (level)
  no operation moved by 1% of the time
where the time goes in v5:
time: 84 us; the launch traced here: 83.5 us
  Pallas kernels  82.7 us (98%)
  between operations  0.84 us (1%)
    pallas_call x1, Pallas kernels, call_layer(): pl.pallas_call(body, name='layer', out_shape=out_shape, in_specs=[any_spe...  79.9 us
    pallas_call x1, Pallas kernels, hand_out(): pl.pallas_call(body, name='hand_out', out_shape=row_shapes + small_shapes...  2.77 us

profile of v5, /device:TPU:0, one launch (start us, length us, event | category | flops | bytes accessed | tf_op | source)
XLA Modules:
  0.0 83.5 jit_solution(13506123326313339843)
XLA Ops:
  0.7 79.9 %layer.1 = (bf16[960,512]{1,0:T(8,128)(2,1)}, bf16[960,512]{1,0:T(8,128)(2,1)}, f32[776,128]{1,0:T(8,128)}) custom-call(bf16[960,512]{1,0:T(8,128)(2,1)} %refs_0_.1, bf16[960,512]{1,0:T(8,128)(2,1)} %refs_1_.1, s32[1,192]{1,0:T(1,128)} %bitcast.33, f32[1,16]{1,0:T(1,128)} %bitcast.34, f32[1,16]{1,0:T(1,128)} %bitcast.35, f32[1,32]{1,0:T(1,128)} %bitcast.36, ...), custom_call_target="tpu_custom_call" | custom-call | flops 18119393280 | bytes 8388608 | tf_op jit(solution)/shard_map/layer/pallas_call | solution.py:841
  80.6 2.8 %hand_out.1 = (bf16[960,512]{1,0:T(8,128)(2,1)}, bf16[960,512]{1,0:T(8,128)(2,1)}, f32[1,16]{1,0:T(1,128)}, f32[1,16]{1,0:T(1,128)}, f32[1,32]{1,0:T(1,128)}, /*...) custom-call(bf16[960,512]{1,0:T(8,128)(2,1)} %get-tuple-element.31.m, ...), custom_call_target="tpu_custom_call" | custom-call | tf_op jit(solution)/shard_map/hand_out/pallas_call | solution.py:887
